TPU v7x, 32 devices: a whole 2x2x4 slice. The times are simulated.
32 devices in a mesh: grp: 2 (over y), row: 4 (over x, core), col: 4 (over z).
Axes of the slice: x: 2, y: 2, z: 4, core: 2. Of those that a mesh axis runs over, the one named last changes fastest.
Arguments:
- grad_out: bfloat16 [512, 8192], P(('grp', 'row'), 'col'), parts along dimension 0, may hold values from -6 to 6
- activations: bfloat16 [512, 28672], P(('grp', 'col'), 'row'), parts along dimension 0, may hold values from -6 to 6
- weight_blocks: bfloat16 [4, 4, 537, 128, 128], P('row', 'col'), may hold values from -0.0625 to 0.0625
- block_ids: int32 [4, 4, 537], P('row', 'col'), may hold values from 0 to 895, as said below
- block_counts: int32 [4, 4], P('row', 'col'), may hold values from 179 to 537, as said below
Outputs:
- grad_hidden: bfloat16 [512, 28672], P(('grp', 'col'), 'row'), parts along dimension 0
- grad_weight: bfloat16 [8, 4, 537, 128, 128], P(('grp', 'row'), 'col'), parts along dimension 0
There are 2 independent parts, one for each index of `grp`. A program takes and returns all parts, laid end to end along the dimension named above; an argument that names none is the same for every part. Nothing has to cross between parts.
Inputs may be any that keep to these rules, and one draw needn't show every extreme that they name: `block_ids`: within one shard the 537 entries are distinct block numbers. `block_counts`: some shard has all 537 slots live in every draw.
All inputs are finite; a program needn't handle non-finite values.
Results may differ from a plain program's by a relative error of at most 0.009.
Values may be sent and summed in bfloat16 or wider, within the bound.
No kernel may reach another device: no remote copies, remote signals or barrier semaphores. Data moves between devices by JAX's collectives and lax.ppermute only.
A program may use at most 448 MiB of HBM per device.

v0:
```python
import jax
import jax.numpy as jnp
from jax import lax
from jax.sharding import PartitionSpec as P

BLOCK = 128


def shards(grad_out, activations, weight_blocks, block_ids, block_counts):
    grad_full = lax.all_gather(grad_out, "row", axis=0, tiled=True)
    tokens = grad_full.shape[0]
    col_blocks = grad_out.shape[1] // BLOCK
    row_blocks = activations.shape[1] // BLOCK
    ids = block_ids[0, 0]
    count = block_counts[0, 0]
    slots = ids.shape[0]
    live = jnp.arange(slots, dtype=jnp.int32) < count
    kept = jnp.where(live[:, None, None], weight_blocks[0, 0], jnp.zeros_like(weight_blocks[0, 0]))
    pick_row = (ids // col_blocks)[:, None] == jnp.arange(row_blocks, dtype=jnp.int32)[None, :]
    pick_col = (ids % col_blocks)[:, None] == jnp.arange(col_blocks, dtype=jnp.int32)[None, :]
    grad_blocks = grad_full.reshape(tokens, col_blocks, BLOCK)
    row_pick = pick_row.astype(jnp.bfloat16)
    row_place = pick_row.astype(jnp.float32)
    chosen_all = jnp.einsum(
        "tcj,sc->tsj",
        grad_blocks,
        pick_col.astype(jnp.bfloat16),
        preferred_element_type=jnp.float32,
    ).astype(jnp.bfloat16)
    chosen = chosen_all
    product = jnp.einsum("tsj,sij->tsi", chosen, kept, preferred_element_type=jnp.float32)
    placed = jnp.einsum("tsi,sb->tbi", product, row_place, precision=lax.Precision.HIGHEST)
    grad_hidden = lax.psum_scatter(
        placed.reshape(lax.axis_size("col") * activations.shape[0], row_blocks * BLOCK).astype(
            jnp.bfloat16
        ),
        "col",
        scatter_dimension=0,
        tiled=True,
    )
    piece = lax.all_gather(activations, "col", axis=0, tiled=True)
    number = piece.shape[0]
    chosen = chosen_all
    hidden_sel = jnp.einsum(
        "tbi,sb->tsi",
        piece.reshape(number, row_blocks, BLOCK),
        row_pick,
        preferred_element_type=jnp.float32,
    ).astype(jnp.bfloat16)
    folded = jnp.einsum("tsi,tsj->sij", hidden_sel, chosen, preferred_element_type=jnp.float32)
    grad_weight = jnp.where(live[:, None, None], folded, jnp.zeros_like(folded)).astype(
        jnp.bfloat16
    )
    return (grad_hidden, grad_weight[None, None])


def solution(mesh):
    placed = (
        P(("grp", "row"), "col"),
        P(("grp", "col"), "row"),
        P("row", "col", None, None, None),
        P("row", "col", None),
        P("row", "col"),
    )
    return jax.shard_map(
        shards,
        mesh=mesh,
        in_specs=placed,
        out_specs=(P(("grp", "col"), "row"), P(("grp", "row"), "col", None, None, None)),
        check_vma=False,
    )
```

profile of v0, /device:TPU:12, one launch (start us, length us, event | category | flops | bytes accessed | tf_op | source)
XLA Modules:
  0.0 305.3 jit_solution(1349455286501714247)
XLA Ops:
  7.2 0.0 all-gather.3.cloned.1.call-start
  7.2 0.7 all-gather.3.cloned.1.call-update
  7.9 0.0 all-gather.5.cloned.1.call-start
  7.9 0.7 all-gather.5.cloned.1.call-update
  8.6 0.0 reduce-scatter.2.cloned.1.call-start
  9.4 0.7 reduce
  10.1 17.4 %all-gather.3.cloned.1.call-done = bf16[256,2048]{1,0:T(8,128)(2,1)} async-done(((bf16[64,2048]{1,0:T(8,128)(2,1)}), bf16[256,2048]{1,0:T(8,128)(2,1)}) %all-gather.3.cloned.1.call-update) | async-done | bytes 1048592 | tf_op jit(solution)/shard_map/all_gather | solution.py:10
  27.4 1.4 copy.11
  28.9 15.4 %convert_bitcast_fusion = bf16[256,537,128]{2,1,0:T(8,128)(2,1)} fusion(bf16[256,16,128]{2,1,0:T(8,128)(2,1)S(1)} %bitcast.42, s32[537]{0:T(1024)S(1)} %get-tuple-element.3), kind=kOutput, calls=%fused_computation.2 | convolution fusion | flops 580690304 | bytes 36243556 | tf_op jit(solution)/shard_map/tcj,sc->tsj/dot_general | solution.py:24
  44.2 48.1 %fusion.5 = f32[537,128,256]{2,1,0:T(8,128)} fusion(bf16[256,537,128]{2,1,0:T(8,128)(2,1)} %convert_bitcast_fusion, bf16[1,1,537,128,128]{4,3,2,1,0:T(8,128)(2,1)} %param.7, pred[537]{0:T(1024)(128)(4,1)S(1)} %iota_compare_fusion.2), kind=kOutput, calls=%fused_computation.7 | convolution fusion | flops 4513480704 | bytes 123175448 | tf_op jit(solution)/shard_map/tsj,sij->tsi/dot_general | solution.py:31
  92.4 64.4 %copy.9 = f32[537,128,256]{1,0,2:T(8,128)} copy(f32[537,128,256]{2,1,0:T(8,128)} %fusion.5) | data formatting | bytes 140771328 | tf_op jit(solution)/shard_map/tsj,sij->tsi/dot_general | solution.py:31
  156.8 34.2 %fusion.15 = bf16[56,256,128]{2,0,1:T(8,128)(2,1)} fusion(f32[537,128,256]{1,0,2:T(8,128)} %copy.9, s32[537]{0:T(1024)S(1)} %get-tuple-element.2), kind=kOutput, calls=%fused_computation.15 | convolution fusion | flops 11826656256 | bytes 74057824 | tf_op jit(solution)/shard_map/tsi,sb->tbi/dot_general | solution.py:32
  191.0 4.6 %copy.22 = bf16[32,8,56,128]{3,1,2,0:T(8,128)(2,1)} copy(bf16[32,8,56,128]{3,2,1,0:T(8,128)(2,1)} %bitcast.41) | data formatting | bytes 7340032
  195.6 0.0 reduce-scatter.2.cloned.1.call-update
  195.6 0.0 all-gather.5.cloned.1.call-done
  195.6 2.8 copy.13
  198.4 15.4 %fusion.19 = bf16[537,256,128]{2,0,1:T(8,128)(2,1)} fusion(bf16[256,56,128]{2,1,0:T(8,128)(2,1)S(1)} %bitcast.39, s32[537]{0:T(1024)S(1)} %get-tuple-element.2), kind=kOutput, calls=%fused_computation.18 | convolution fusion | flops 1970828672 | bytes 38864996 | tf_op jit(solution)/shard_map/tbi,sb->tsi/dot_general | solution.py:44
  213.8 48.4 %copy.10 = bf16[537,256,128]{1,2,0:T(8,128)(2,1)} copy(bf16[537,256,128]{2,0,1:T(8,128)(2,1)} %fusion.19) | data formatting | bytes 70385664 | tf_op jit(solution)/shard_map/tbi,sb->tsi/dot_general | solution.py:44
  262.2 36.5 %fusion.8 = bf16[1,1,537,128,128]{4,3,2,1,0:T(8,128)(2,1)} fusion(pred[537]{0:T(1024)(128)(4,1)S(1)} %iota_compare_fusion.2, bf16[256,537,128]{2,1,0:T(8,128)(2,1)} %convert_bitcast_fusion, bf16[537,256,128]{1,2,0:T(8,128)(2,1)} %copy.10), kind=kOutput, calls=%fused_computation.10 | convolution fusion | flops 4522278912 | bytes 87982616 | tf_op jit(solution)/shard_map/tsi,tsj->sij/dot_general | solution.py:50
  298.8 0.0 reduce-scatter.2.cloned.1.call-done
  (2 shorter events, 0.0 us)
Async XLA Ops:
  7.2 20.3 %all-gather.3.cloned.1.call-start = ((), (), s32[]{:S(2)}) async-start(), calls=%async_computation.1 | async-start | bytes 1310720 | tf_op jit(solution)/shard_map/all_gather | solution.py:10
  7.9 187.7 %all-gather.5.cloned.1.call-start = ((), (), s32[]{:S(2)}) async-start(), calls=%async_computation.3 | async-start | bytes 4587520 | tf_op jit(solution)/shard_map/all_gather | solution.py:41
  8.6 290.1 %reduce-scatter.2.cloned.1.call-start = ((), (), s32[]{:S(2)}) async-start(), calls=%async_computation.2 | async-start | bytes 4587520 | tf_op jit(solution)/shard_map/reduce_scatter | solution.py:33
Sparse Core Ops, SparseCore 0:
  9.6 17.8 all-gather.2
  29.0 69.7 all-gather.4
  195.7 68.2 reduce-scatter.1
where the time goes:
time: 309 us; the launch traced here: 305 us
  matrix products  150 us (49%)
  local copies, waits for them, and re-layouts  122 us (39%)
  waiting for transfers between devices  18.8 us (6%)
  between operations  14.4 us (5%)
    dot_general x1, local copies, waits for them, and re-layouts, shards(): jnp.einsum('tsj,sij->tsi', chosen, kept, preferred_element_type=jnp.float32)  64.4 us
    dot_general x1, local copies, waits for them, and re-layouts, shards(): jnp.einsum('tbi,sb->tsi', piece.reshape(number, row_blocks, BLOCK), row_p...  48.4 us
    dot_general x1, matrix products, shards(): jnp.einsum('tsj,sij->tsi', chosen, kept, preferred_element_type=jnp.float32)  48.1 us
    dot_general x1, matrix products, shards(): jnp.einsum('tsi,tsj->sij', hidden_sel, chosen, preferred_element_type=jnp...  36.5 us
    dot_general x1, matrix products, shards(): jnp.einsum('tsi,sb->tbi', product, row_place, precision=lax.Precision.HIG...  34.2 us
    all_gather x1, waiting for transfers between devices, shards(): grad_full = lax.all_gather(grad_out, 'row', axis=0, tiled=True)  17.4 us
    dot_general x1, matrix products, shards(): jnp.einsum('tbi,sb->tsi', piece.reshape(number, row_blocks, BLOCK), row_p...  15.4 us
    dot_general x1, matrix products, shards(): jnp.einsum('tcj,sc->tsj', grad_blocks, pick_col.astype(jnp.bfloat16), pre...  15.4 us
  transfers between devices with their start and end apart: 3, of which 1 were waited for; matrix products, arithmetic and copies ran while one was open for 89% of the time, Pallas kernels for 0%

commit v1 on v0

v1 whole, which is shorter than its diff:
```python
import functools

import jax
import jax.numpy as jnp
from jax import lax
from jax.experimental import pallas as pl
from jax.experimental.pallas import tpu as pltpu
from jax.sharding import PartitionSpec as P

BLOCK = 128
CHUNKS = 2
MIB = 1 << 20
SMEM = pl.BlockSpec(memory_space=pltpu.SMEM)
VMEM = pl.BlockSpec(memory_space=pltpu.VMEM)
ANY = pl.BlockSpec(memory_space=pl.ANY)


def partial_body(chunk, tile, slot_of, grads, blocks, out):
    cols, high = grads.shape[1] // BLOCK, tile // BLOCK

    def block(r, c):
        slot = slot_of[(chunk * (out.shape[1] // BLOCK) + r) * cols + c]
        held = blocks[jnp.maximum(slot, 0)]
        return jnp.where(slot >= 0, held, jnp.zeros_like(held))

    def step(i, carry):
        weights = jnp.concatenate(
            [jnp.concatenate([block(i * high + p, c) for c in range(cols)], 1) for p in range(high)], 0
        )
        out[:, pl.ds(pl.multiple_of(i * tile, tile), tile)] = lax.dot_general(
            grads[...], weights, (((1,), (1,)), ((), ())), preferred_element_type=jnp.float32
        ).astype(out.dtype)
        return carry

    lax.fori_loop(0, out.shape[1] // tile, step, 0)


def first_partial_kernel(tile, masks, slot_of, me, *refs):
    pieces, (blocks, out, grads) = refs[: len(masks)], refs[len(masks) :]
    rows = pieces[0].shape[0]
    for mask, piece in zip(masks, pieces):
        at = pl.multiple_of((me[0] ^ mask) * rows, rows)
        grads[pl.ds(at, rows), :] = piece[...]
    partial_body(0, tile, slot_of, grads, blocks, out)


def partial_kernel(chunk, tile, slot_of, grads, blocks, out):
    partial_body(chunk, tile, slot_of, grads, blocks, out)


def weight_grad_kernel(chunk, tile, n, slot_of, where, count, own, grads, *refs):
    flows = refs[: n - 1], refs[n - 1 : 2 * n - 2]
    refs = refs[2 * n - 2 :]
    if chunk:
        refs = refs[1:]
    out, done, acts, dense, zero, act_sem, sem = refs
    me = where[0]
    rows, cols = dense.shape[0], dense.shape[1]
    part, width = acts.shape[0] // n, acts.shape[1]

    def spot(i):
        return acts.at[pl.ds(pl.multiple_of(i * part, part), part), :]

    copies = [(None, pltpu.make_async_copy(own.at[:, pl.ds(chunk * width, width)], spot(me), act_sem))]
    for e, flow in enumerate(flows):
        from_left = (me + e) % 2 == 1
        for j in range(n - 1):
            owner = jnp.where(from_left, me - 1 - j, me + 1 + j)
            needed = (owner >= 0) & (owner < n)
            copies.append((needed, pltpu.make_async_copy(flow[j], spot(jnp.clip(owner, 0, n - 1)), act_sem)))
    for method in ("start", "wait"):
        for needed, copy in copies:
            if needed is None:
                getattr(copy, method)()
            else:
                pl.when(needed)(getattr(copy, method))
        if method == "start" and chunk == 0:
            zero[...] = jnp.zeros_like(zero)

            def clear(slot, carry):
                pltpu.make_async_copy(zero, out.at[slot], sem).start()
                return carry

            lax.fori_loop(count[0], out.shape[0], clear, 0)

    wide = min(512, grads.shape[1])

    def step(i, live):
        turned = acts[:, pl.ds(pl.multiple_of(i * tile, tile), tile)].T
        for j in range(0, grads.shape[1], wide):
            product = jnp.dot(turned, grads[:, j : j + wide], preferred_element_type=jnp.float32).astype(dense.dtype)
            for p in range(tile // BLOCK):
                for q in range(wide // BLOCK):
                    dense[i * (tile // BLOCK) + p, j // BLOCK + q] = product[
                        p * BLOCK : (p + 1) * BLOCK, q * BLOCK : (q + 1) * BLOCK
                    ]
        for p in range(tile // BLOCK):
            for c in range(cols):
                r = i * (tile // BLOCK) + p
                slot = slot_of[(chunk * rows + r) * cols + c]

                @pl.when(slot >= 0)
                def _():
                    pltpu.make_async_copy(dense.at[r, c], out.at[slot], sem).start()

                live = live + (slot >= 0).astype(jnp.int32)
        return live

    live = lax.fori_loop(0, rows * BLOCK // tile, step, jnp.int32(0))
    if chunk == 0:
        live = live + out.shape[0] - count[0]

    def drain(i, carry):
        pltpu.make_async_copy(dense.at[0, 0], out.at[0], sem).wait()
        return carry

    lax.fori_loop(0, live, drain, 0)
    done[0] = live


def params(mib):
    return pltpu.CompilerParams(vmem_limit_bytes=mib * MIB)


def cost(flops, moved):
    return pl.CostEstimate(flops=flops, bytes_accessed=moved, transcendentals=0)


def shards(grad_out, activations, weight_blocks, block_ids, block_counts):
    R, n = lax.axis_size("row"), lax.axis_size("col")
    r, c = lax.axis_index("row"), lax.axis_index("col")
    rows_g, depth = grad_out.shape
    part, hidden = activations.shape
    tokens = n * part
    width = hidden // CHUNKS
    col_blocks, row_blocks = depth // BLOCK, hidden // BLOCK
    tile = width // 2 if width % (2 * BLOCK) == 0 else width
    slots = block_ids.shape[-1]
    kind = grad_out.dtype
    first = [(i, i ^ 1) for i in range(n)]
    second = [(i, i + 1) for i in range(1, n - 1, 2)] + [(i + 1, i) for i in range(1, n - 1, 2)]
    links = (first, second)
    even = c % 2 == 0
    right_going = (even, jnp.logical_not(even))
    origin = [jnp.where(goes, c, n - 1 - c) for goes in right_going]

    ids, count = block_ids[0, 0], block_counts[0]
    number = jnp.arange(slots, dtype=jnp.int32)
    held = (ids[:, None] == jnp.arange(row_blocks * col_blocks, dtype=jnp.int32)) & (number < count)[:, None]
    slot_of = jnp.max(jnp.where(held, number[:, None], -1), axis=0)

    pieces, masks = [grad_out], [0]
    bit = R // 2
    while bit:
        pairs = [(i, i ^ bit) for i in range(R)]
        pieces = pieces + [lax.ppermute(piece, "row", pairs) for piece in pieces]
        masks = masks + [mask ^ bit for mask in masks]
        bit //= 2

    blocks = weight_blocks[0, 0]
    work = cost(2 * tokens * width * depth, 2 * width * depth)
    sums, grads = pl.pallas_call(
        functools.partial(first_partial_kernel, tile, masks),
        out_shape=[jax.ShapeDtypeStruct((tokens, width), kind), jax.ShapeDtypeStruct((tokens, depth), kind)],
        in_specs=[SMEM, SMEM] + [VMEM] * (R + 1),
        out_specs=[VMEM, VMEM],
        compiler_params=params(16),
        cost_estimate=work,
        name="partial0",
    )(slot_of, r[None].astype(jnp.int32), *pieces, blocks)
    partial = [sums]

    def add_partial(h, slot_of):
        partial.append(
            pl.pallas_call(
                functools.partial(partial_kernel, h, tile),
                out_shape=jax.ShapeDtypeStruct((tokens, width), kind),
                in_specs=[SMEM, VMEM, VMEM],
                out_specs=VMEM,
                compiler_params=params(16),
                cost_estimate=work,
                name=f"partial{h}",
            )(slot_of, grads, blocks)
        )

    def rows_of(h, d):
        return lax.dynamic_slice_in_dim(partial[h], jnp.clip(d, 0, n - 1) * part, part, 0)

    def weight_grad(h, slot_of, out):
        flows = [came[h][e][j] for e in range(2) for j in range(n - 1)]
        given = [slot_of, c[None].astype(jnp.int32), count, activations, grads, *flows]
        specs = [SMEM, SMEM, SMEM, ANY, VMEM] + [ANY] * (2 * n - 2)
        if h:
            given.append(out)
            specs.append(ANY)
        return pl.pallas_call(
            functools.partial(weight_grad_kernel, h, tile, n),
            out_shape=[jax.ShapeDtypeStruct((slots, BLOCK, BLOCK), kind), jax.ShapeDtypeStruct((1,), jnp.int32)],
            in_specs=specs,
            out_specs=[ANY, SMEM],
            scratch_shapes=[
                pltpu.VMEM((tokens, width), kind),
                pltpu.VMEM((row_blocks // CHUNKS, col_blocks, BLOCK, BLOCK), kind),
                pltpu.VMEM((BLOCK, BLOCK), kind),
                pltpu.SemaphoreType.DMA,
                pltpu.SemaphoreType.DMA,
            ],
            input_output_aliases={len(given) - 1: 0} if h else {},
            compiler_params=params(20),
            cost_estimate=cost(2 * tokens * width * depth, 2 * weight_blocks.size // CHUNKS),
            name=f"weight_grad{h}",
        )(*given)

    came = [[[] for _ in links] for _ in range(CHUNKS)]
    out = done = None
    for k in range(n):
        for h in range(CHUNKS):
            messages = []
            for e in range(len(links)):
                if k == 0:
                    message = activations[:, h * width : (h + 1) * width]
                else:
                    last = came[h][1 - e][k - 1]
                    if done is not None:
                        last, _ = lax.optimization_barrier((last, done))
                    d = jnp.where(right_going[e], n - k + origin[e], k - 1 - origin[e])
                    message = jnp.where(
                        k <= origin[e], last, rows_of(h, d) + jnp.where(origin[e] > 0, last, jnp.zeros_like(last))
                    )
                messages.append(message)
            for e, pairs in enumerate(links):
                came[h][e].append(lax.ppermute(messages[e], "col", pairs))
            after, _ = lax.optimization_barrier((slot_of, messages))
            if k == 1 and h + 1 < CHUNKS:
                add_partial(h + 1, after)
            if k == n - 1:
                out, done = weight_grad(h, after, out)

    hidden_parts = []
    inner = (c > 0) & (c < n - 1)
    for h in range(CHUNKS):
        mine, _ = lax.optimization_barrier((rows_of(h, c), done))
        total = mine.astype(jnp.float32) + came[h][0][n - 1].astype(jnp.float32)
        total = total + jnp.where(inner, came[h][1][n - 1], jnp.zeros_like(came[h][1][n - 1])).astype(jnp.float32)
        hidden_parts.append(total.astype(kind))
    return jnp.concatenate(hidden_parts, 1), out[None, None]


def solution(mesh):
    placed = (
        P(("grp", "row"), "col"),
        P(("grp", "col"), "row"),
        P("row", "col", None, None, None),
        P("row", "col", None),
        P("row", "col"),
    )
    return jax.shard_map(
        shards,
        mesh=mesh,
        in_specs=placed,
        out_specs=(P(("grp", "col"), "row"), P(("grp", "row"), "col", None, None, None)),
        check_vma=False,
    )
```

time: 309 us -> 101 us (0.33)
  matrix products: 150 us -> 0 us
  local copies, waits for them, and re-layouts: 122 us -> 13.2 us
  Pallas kernels: 0 us -> 29.9 us
  starting transfers between devices: 0.11 us -> 25.8 us
  between operations: 14.4 us -> 1.79 us
  other arithmetic: 0.72 us -> 7.15 us
    dot_general x5 -> x0, matrix products: 150 us -> none  [the longest x1 48.1 us: shards(): jnp.einsum('tsj,sij->tsi', chosen, kept, preferred_element_type=jnp.float32)]
    dot_general x2 -> x0, local copies, waits for them, and re-layouts: 113 us -> none  [the longest x1 64.4 us: shards(): jnp.einsum('tsj,sij->tsi', chosen, kept, preferred_element_type=jnp.float32)]
    pallas_call x0 -> x4, Pallas kernels: none -> 29.9 us  [the longest x2 19.8 us: weight_grad(): pl.pallas_call(functools.partial(weight_grad_kernel, h, tile, n), out_sha...]
    ppermute x0 -> x19, starting transfers between devices: none -> 25.8 us  [the longest x16 24.2 us: shards(): came[h][e].append(lax.ppermute(messages[e], 'col', pairs))]
    ppermute x0 -> x19, waiting for transfers between devices: none -> 21.6 us  [the longest x16 21.6 us: shards(): came[h][e].append(lax.ppermute(messages[e], 'col', pairs))]
    all_gather x2 -> x0, waiting for transfers between devices: 17.4 us -> none  [the longest x1 17.4 us: shards(): grad_full = lax.all_gather(grad_out, 'row', axis=0, tiled=True)]
    unnamed x3 -> x38, local copies, waits for them, and re-layouts: 8.82 us -> 11.1 us
  transfers between devices with their start and end apart: 3 -> 19, of which waited for: 1 -> 6; matrix products, arithmetic and copies ran while one was open for 89% -> 7% of each run, Pallas kernels for 0% -> 30%
where the time goes in v1:
time: 101 us; the launch traced here: 99.5 us
  Pallas kernels  29.9 us (30%)
  starting transfers between devices  25.8 us (26%)
  waiting for transfers between devices  21.6 us (21%)
  local copies, waits for them, and re-layouts  13.2 us (13%)
  other arithmetic  7.15 us (7%)
  between operations  1.79 us (2%)
    ppermute x16, starting transfers between devices, shards(): came[h][e].append(lax.ppermute(messages[e], 'col', pairs))  24.2 us
    ppermute x16, waiting for transfers between devices, shards(): came[h][e].append(lax.ppermute(messages[e], 'col', pairs))  21.6 us
    pallas_call x2, Pallas kernels, weight_grad(): pl.pallas_call(functools.partial(weight_grad_kernel, h, tile, n), out_sha...  19.8 us
    unnamed x38, local copies, waits for them, and re-layouts  11.1 us
    pallas_call x1, Pallas kernels, shards(): pl.pallas_call(functools.partial(first_partial_kernel, tile, masks), out_...  5.06 us
    pallas_call x1, Pallas kernels, add_partial(): pl.pallas_call(functools.partial(partial_kernel, h, tile), out_shape=jax....  4.99 us
    select_n x5, other arithmetic, shards(): jnp.where(k <= origin[e], last, rows_of(h, d) + jnp.where(origin[e] > 0,...  2.71 us
    slice x1, local copies, waits for them, and re-layouts, shards(): message = activations[:, h * width:(h + 1) * width]  2.13 us
  transfers between devices with their start and end apart: 19, of which 6 were waited for; matrix products, arithmetic and copies ran while one was open for 7% of the time, Pallas kernels for 30%

profile of v1, /device:TPU:12, one launch (start us, length us, event | category | flops | bytes accessed | tf_op | source)
XLA Modules:
  0.0 99.5 jit_solution(14595826148410688206)
XLA Ops:
  0.6 0.0 copy-start.13
  0.6 1.6 %collective-permute-start = (bf16[64,2048]{1,0:T(8,128)(2,1)}, bf16[64,2048]{1,0:T(8,128)(2,1)S(1)}, u32[]{:S(2)}, u32[]{:S(2)}) collective-permute-start(bf16[64,2048]{1,0:T(8,128)(2,1)} %refs_0_.1), channel_id=1, source_target_pairs={{0,8},{4,12},{8,0},{12,4},{1,9},{5,13},{9,1},{13,5},{2,10},{6,14},... | collective-permute-start | bytes 786440 | tf_op jit(solution)/shard_map/ppermute | solution.py:156
  2.2 0.0 collective-permute-start.1
  2.2 2.1 %fusion.1 = (bf16[64,3584]{1,0:T(8,128)(2,1)}, bf16[64,3584]{1,0:T(8,128)(2,1)}) fusion(bf16[64,7168]{1,0:T(8,128)(2,1)} %own.3), kind=kLoop, calls=%fused_computation.21 | loop fusion | bytes 1835008 | tf_op jit(solution)/shard_map/slice | solution.py:221
  4.3 0.4 collective-permute-start.5
  4.8 4.6 %collective-permute-start.4 = (bf16[64,3584]{1,0:T(8,128)(2,1)}, bf16[64,3584]{1,0:T(8,128)(2,1)S(1)}, u32[]{:S(2)}, u32[]{:S(2)}) collective-permute-start(bf16[64,3584]{1,0:T(8,128)(2,1)} %get-tuple-element.42), channel_id=1, source_target_pairs={{1,2},{2,1},{5,6},{6,5},{9,10},{10,9},{13,14},{14,13},{17,18},{18,... | collective-permute-start | bytes 1376264 | tf_op jit(solution)/shard_map/ppermute | solution.py:232
  9.4 0.1 collective-permute-start.12
  10.2 0.0 collective-permute-done.refs_1_
  10.2 0.1 collective-permute-start.2
  10.3 0.5 select_reduce_fusion.slot_of
  10.9 0.0 collective-permute-done.1.refs_2_
  10.9 0.7 copy-done.14
  11.6 2.1 %collective-permute-start.3 = (bf16[64,3584]{1,0:T(8,128)(2,1)}, bf16[64,3584]{1,0:T(8,128)(2,1)S(1)}, u32[]{:S(2)}, u32[]{:S(2)}) collective-permute-start(bf16[64,3584]{1,0:T(8,128)(2,1)} %get-tuple-element.43), channel_id=1, source_target_pairs={{1,2},{2,1},{5,6},{6,5},{9,10},{10,9},{13,14},{14,13},{17,18},{18,... | collective-permute-start | bytes 1376264 | tf_op jit(solution)/shard_map/ppermute | solution.py:232
  13.7 0.0 collective-permute-done.2.refs_3_
  13.7 0.0 copy-start
  13.7 6.0 %copy-done = bf16[1,1,537,128,128]{4,3,2,1,0:T(8,128)(2,1)S(1)} copy-done((bf16[1,1,537,128,128]{4,3,2,1,0:T(8,128)(2,1)S(1)}, bf16[1,1,537,128,128]{4,3,2,1,0:T(8,128)(2,1)}, u32[]{:S(2)}) %copy-start) | copy-done | bytes 17596440
  19.7 0.9 copy-done.15
  20.7 5.1 %partial0.1 = (bf16[256,3584]{1,0:T(8,128)(2,1)S(1)}, bf16[256,2048]{1,0:T(8,128)(2,1)S(1)}) custom-call(s32[896]{0:T(1024)S(1)} %select_reduce_fusion.slot_of, s32[1]{0:T(128)} %bitcast.1.me, bf16[64,2048]{1,0:T(8,128)(2,1)S(1)} %copy-done.13, bf16[64,2048]{1,0:T(8,128)(2,1)S(1)} %collective-permute-done.refs_1_, bf16[64,2048]{1,0:T(8,128)(2,1)S(1)} %copy-done.15, ...), custom_call_target="tpu_custom_call" | custom-call | flops 3758096384 | bytes 14680064 | tf_op jit(solution)/shard_map/partial0/pallas_call | solution.py:162
  25.7 0.0 collective-permute-done.5.refs_0_
  25.8 0.0 collective-permute-done.4.refs_3_
  25.8 0.0 copy-start.11
  25.8 0.4 add_select_fusion.10
  26.2 3.7 %collective-permute-start.10 = (bf16[64,3584]{1,0:T(8,128)(2,1)S(1)}, bf16[64,3584]{1,0:T(8,128)(2,1)S(1)}, u32[]{:S(2)}, u32[]{:S(2)}) collective-permute-start(bf16[64,3584]{1,0:T(8,128)(2,1)S(1)} %get-tuple-element.40), channel_id=1, source_target_pairs={{1,2},{2,1},{5,6},{6,5},{9,10},{10,9},{13,14},{14,13},{17,18},{18,... | collective-permute-start | bytes 1376264 | tf_op jit(solution)/shard_map/ppermute | solution.py:232
  29.9 0.1 collective-permute-start.8
  30.0 0.0 copy-done.1
  30.0 5.0 %partial1.1 = bf16[256,3584]{1,0:T(8,128)(2,1)S(1)} custom-call(s32[896]{0:T(1024)S(1)} %select_reduce_fusion.slot_of, bf16[256,2048]{1,0:T(8,128)(2,1)S(1)} %get-tuple-element.17.grads, bf16[537,128,128]{2,1,0:T(8,128)(2,1)S(1)} %bitcast.10), custom_call_target="tpu_custom_call" | custom-call | flops 3758096384 | bytes 14680064 | tf_op jit(solution)/shard_map/partial1/pallas_call | solution.py:175
  35.0 0.0 collective-permute-done.12.refs_0_
  35.0 0.0 collective-permute-done.3.refs_3_
  35.0 0.3 add_select_fusion.2
  35.4 2.1 %collective-permute-start.13 = (bf16[64,3584]{1,0:T(8,128)(2,1)S(1)}, bf16[64,3584]{1,0:T(8,128)(2,1)S(1)}, u32[]{:S(2)}, u32[]{:S(2)}) collective-permute-start(bf16[64,3584]{1,0:T(8,128)(2,1)S(1)} %get-tuple-element.36), channel_id=1, source_target_pairs={{1,2},{2,1},{5,6},{6,5},{9,10},{10,9},{13,14},{14,13},{17,18},{18,... | collective-permute-start | bytes 1376264 | tf_op jit(solution)/shard_map/ppermute | solution.py:232
  37.5 0.6 collective-permute-start.6
  38.1 3.3 %collective-permute-done.10.refs_4_ = bf16[64,3584]{1,0:T(8,128)(2,1)S(1)} collective-permute-done((bf16[64,3584]{1,0:T(8,128)(2,1)S(1)}, bf16[64,3584]{1,0:T(8,128)(2,1)S(1)}, u32[]{:S(2)}, u32[]{:S(2)}) %collective-permute-start.10) | collective-permute-done | bytes 458784 | tf_op jit(solution)/shard_map/ppermute | solution.py:232
  41.4 1.9 %collective-permute-done.8.refs_1_ = bf16[64,3584]{1,0:T(8,128)(2,1)S(1)} collective-permute-done((bf16[64,3584]{1,0:T(8,128)(2,1)S(1)}, bf16[64,3584]{1,0:T(8,128)(2,1)S(1)}, u32[]{:S(2)}, u32[]{:S(2)}) %collective-permute-start.8) | collective-permute-done | bytes 458784 | tf_op jit(solution)/shard_map/ppermute | solution.py:232
  43.3 0.3 add_select_fusion.5
  43.7 0.1 collective-permute-start.11
  43.8 2.1 %collective-permute-start.9 = (bf16[64,3584]{1,0:T(8,128)(2,1)S(1)}, bf16[64,3584]{1,0:T(8,128)(2,1)S(1)}, u32[]{:S(2)}, u32[]{:S(2)}) collective-permute-start(bf16[64,3584]{1,0:T(8,128)(2,1)S(1)} %get-tuple-element.39), channel_id=1, source_target_pairs={{1,2},{2,1},{5,6},{6,5},{9,10},{10,9},{13,14},{14,13},{17,18},{18,... | collective-permute-start | bytes 1376264 | tf_op jit(solution)/shard_map/ppermute | solution.py:232
  45.9 5.3 %collective-permute-done.13.refs_4_ = bf16[64,3584]{1,0:T(8,128)(2,1)S(1)} collective-permute-done((bf16[64,3584]{1,0:T(8,128)(2,1)S(1)}, bf16[64,3584]{1,0:T(8,128)(2,1)S(1)}, u32[]{:S(2)}, u32[]{:S(2)}) %collective-permute-start.13) | collective-permute-done | bytes 458784 | tf_op jit(solution)/shard_map/ppermute | solution.py:232
  51.2 1.9 %collective-permute-done.6.refs_1_ = bf16[64,3584]{1,0:T(8,128)(2,1)S(1)} collective-permute-done((bf16[64,3584]{1,0:T(8,128)(2,1)S(1)}, bf16[64,3584]{1,0:T(8,128)(2,1)S(1)}, u32[]{:S(2)}, u32[]{:S(2)}) %collective-permute-start.6) | collective-permute-done | bytes 458784 | tf_op jit(solution)/shard_map/ppermute | solution.py:232
  53.2 0.3 add_select_fusion.1
  53.5 0.1 collective-permute-start.14
  53.6 0.4 copy-done.3
  54.0 2.2 %collective-permute-start.7 = (bf16[64,3584]{1,0:T(8,128)(2,1)S(1)}, bf16[64,3584]{1,0:T(8,128)(2,1)S(1)}, u32[]{:S(2)}, u32[]{:S(2)}) collective-permute-start(bf16[64,3584]{1,0:T(8,128)(2,1)S(1)} %get-tuple-element.35), channel_id=1, source_target_pairs={{1,2},{2,1},{5,6},{6,5},{9,10},{10,9},{13,14},{14,13},{17,18},{18,... | collective-permute-start | bytes 1376264 | tf_op jit(solution)/shard_map/ppermute | solution.py:232
  56.2 6.8 %collective-permute-done.11.refs_2_ = bf16[64,3584]{1,0:T(8,128)(2,1)S(1)} collective-permute-done((bf16[64,3584]{1,0:T(8,128)(2,1)S(1)}, bf16[64,3584]{1,0:T(8,128)(2,1)S(1)}, u32[]{:S(2)}, u32[]{:S(2)}) %collective-permute-start.11) | collective-permute-done | bytes 458784 | tf_op jit(solution)/shard_map/ppermute | solution.py:232
  63.0 0.0 collective-permute-done.9.refs_5_
  63.0 1.3 %constant_dynamic-slice_fusion.1 = (bf16[64,3584]{1,0:T(8,128)(2,1)}, bf16[64,3584]{1,0:T(8,128)(2,1)}, bf16[64,3584]{1,0:T(8,128)(2,1)}) fusion(bf16[256,3584]{1,0:T(8,128)(2,1)S(1)} %get-tuple-element.15, s32[]{:T(128)S(6)} %select_n.194, bf16[64,3584]{1,0:T(8,128)(2,1)S(1)} %collective-permute-done.11.refs_2_, pred[]{:T(512)S(6)} %gt.7, ...), kind=kLoop, calls=%fused_computation.20 | loop fusion | flops 2752512 | bytes 3670032 | tf_op jit(solution)/shard_map/dynamic_slice | solution.py:187
  64.3 11.8 %weight_grad0.1 = (bf16[537,128,128]{2,1,0:T(8,128)(2,1)}, s32[1]{0:T(128)}) custom-call(s32[896]{0:T(1024)S(1)} %select_reduce_fusion.slot_of, s32[1]{0:T(128)} %bitcast.3.where, s32[1]{0:T(128)} %bitcast.7.count, bf16[64,7168]{1,0:T(8,128)(2,1)S(1)} %copy-done.2, bf16[256,2048]{1,0:T(8,128)(2,1)S(1)} %get-tuple-element.17.grads, ...), custom_call_target="tpu_custom_call" | custom-call | flops 3758096384 | bytes 8798208 | tf_op jit(solution)/shard_map/weight_grad0/pallas_call | solution.py:196
  76.1 0.0 collective-permute-done.14.refs_2_
  76.1 0.0 collective-permute-done.7.refs_5_
  76.1 1.3 %add_select_fusion = (bf16[64,3584]{1,0:T(8,128)(2,1)}, bf16[64,3584]{1,0:T(8,128)(2,1)}, bf16[64,3584]{1,0:T(8,128)(2,1)}) fusion(bf16[64,3584]{1,0:T(8,128)(2,1)S(1)} %collective-permute-done.14.refs_2_, bf16[256,3584]{1,0:T(8,128)(2,1)S(1)} %partial1.1, s32[]{:T(128)S(6)} %select_n.231, pred[]{:T(512)S(6)} %ge.28, pred[]{:T(512)S(6)} %gt.7, ...), kind=kLoop, calls=%fused_computation.6 | loop fusion | flops 2752512 | bytes 3670032 | tf_op jit(solution)/shard_map/jit(_where)/select_n | solution.py:227
  77.5 0.0 collective-permute-start.17
  77.5 1.9 %collective-permute-start.18 = (bf16[64,3584]{1,0:T(8,128)(2,1)}, bf16[64,3584]{1,0:T(8,128)(2,1)}, u32[]{:S(2)}, u32[]{:S(2)}) collective-permute-start(bf16[64,3584]{1,0:T(8,128)(2,1)} %get-tuple-element.31), channel_id=1, source_target_pairs={{1,2},{2,1},{5,6},{6,5},{9,10},{10,9},{13,14},{14,13},{17,18},{18,... | collective-permute-start | bytes 1376264 | tf_op jit(solution)/shard_map/ppermute | solution.py:232
  79.4 1.5 %collective-permute-start.15 = (bf16[64,3584]{1,0:T(8,128)(2,1)}, bf16[64,3584]{1,0:T(8,128)(2,1)S(1)}, u32[]{:S(2)}, u32[]{:S(2)}) collective-permute-start(bf16[64,3584]{1,0:T(8,128)(2,1)} %get-tuple-element.30), channel_id=1, source_target_pairs={{0,1},{1,0},{2,3},{3,2},{4,5},{5,4},{6,7},{7,6},{8,9},{9,8},{10,11... | collective-permute-start | bytes 1376264 | tf_op jit(solution)/shard_map/ppermute | solution.py:232
  80.9 2.5 %collective-permute-start.16 = (bf16[64,3584]{1,0:T(8,128)(2,1)}, bf16[64,3584]{1,0:T(8,128)(2,1)S(1)}, u32[]{:S(2)}, u32[]{:S(2)}) collective-permute-start(bf16[64,3584]{1,0:T(8,128)(2,1)} %get-tuple-element.29), channel_id=1, source_target_pairs={{1,2},{2,1},{5,6},{6,5},{9,10},{10,9},{13,14},{14,13},{17,18},{18,... | collective-permute-start | bytes 1376264 | tf_op jit(solution)/shard_map/ppermute | solution.py:232
  83.4 1.0 %copy-done.4 = bf16[64,3584]{1,0:T(8,128)(2,1)S(1)} copy-done((bf16[64,3584]{1,0:T(8,128)(2,1)S(1)}, bf16[64,3584]{1,0:T(8,128)(2,1)}, u32[]{:S(2)}) %copy-start.4) | copy-done | bytes 458776
  84.4 1.0 %copy-done.6 = bf16[64,3584]{1,0:T(8,128)(2,1)S(1)} copy-done((bf16[64,3584]{1,0:T(8,128)(2,1)S(1)}, bf16[64,3584]{1,0:T(8,128)(2,1)}, u32[]{:S(2)}) %copy-start.6) | copy-done | bytes 458776
  85.5 1.0 %copy-done.8 = bf16[64,3584]{1,0:T(8,128)(2,1)S(1)} copy-done((bf16[64,3584]{1,0:T(8,128)(2,1)S(1)}, bf16[64,3584]{1,0:T(8,128)(2,1)}, u32[]{:S(2)}) %copy-start.8) | copy-done | bytes 458776
  86.5 8.1 %weight_grad1.1 = (bf16[537,128,128]{2,1,0:T(8,128)(2,1)}, s32[1]{0:T(128)}) custom-call(s32[896]{0:T(1024)S(1)} %select_reduce_fusion.slot_of, s32[1]{0:T(128)} %bitcast.3.where, s32[1]{0:T(128)} %bitcast.8.count, bf16[64,7168]{1,0:T(8,128)(2,1)S(1)} %copy-done.2, bf16[256,2048]{1,0:T(8,128)(2,1)S(1)} %get-tuple-element.17.grads, ...), custom_call_target="tpu_custom_call", output_to_operand_aliasing={{0}: (11, {})} | custom-call | flops 3758096384 | bytes 8798208 | tf_op jit(solution)/shard_map/weight_grad1/pallas_call | solution.py:196
  94.6 0.0 collective-permute-done.17
  94.6 0.0 collective-permute-done.18
  94.6 1.4 %add_convert_fusion = bf16[64,3584]{1,0:T(8,128)(2,1)S(1)} fusion(bf16[64,3584]{1,0:T(8,128)(2,1)} %collective-permute-done.17, bf16[64,3584]{1,0:T(8,128)(2,1)S(1)} %copy-done.17, bf16[64,3584]{1,0:T(8,128)(2,1)} %collective-permute-done.18, pred[]{:T(512)S(6)} %and.21), kind=kLoop, calls=%fused_computation.4 | loop fusion | flops 1605632 | bytes 1835009 | tf_op jit(solution)/shard_map/convert_element_type | solution.py:245
  96.0 0.0 collective-permute-done.15
  96.0 2.3 %collective-permute-done.16 = bf16[64,3584]{1,0:T(8,128)(2,1)S(1)} collective-permute-done((bf16[64,3584]{1,0:T(8,128)(2,1)}, bf16[64,3584]{1,0:T(8,128)(2,1)S(1)}, u32[]{:S(2)}, u32[]{:S(2)}) %collective-permute-start.16) | collective-permute-done | bytes 458784 | tf_op jit(solution)/shard_map/ppermute | solution.py:232
  98.3 0.2 add_convert_fusion.1
  98.5 1.0 pad_maximum_fusion
  (29 shorter events, 0.1 us)
Async XLA Ops:
  0.6 13.1 %copy-start.13 = (bf16[64,2048]{1,0:T(8,128)(2,1)S(1)}, bf16[64,2048]{1,0:T(8,128)(2,1)}, u32[]{:S(2)}) copy-start(bf16[64,2048]{1,0:T(8,128)(2,1)} %refs_0_.1) | copy-start | bytes 786436
  0.6 8.9 %copy-start.18 = (s32[1,1,537]{2,1,0:T(1,128)S(1)}, s32[1,1,537]{2,1,0:T(1,128)}, u32[]{:S(2)}) copy-start(s32[1,1,537]{2,1,0:T(1,128)} %param.8) | copy-start | bytes 6448
  0.6 9.6 %collective-permute-start = (bf16[64,2048]{1,0:T(8,128)(2,1)}, bf16[64,2048]{1,0:T(8,128)(2,1)S(1)}, u32[]{:S(2)}, u32[]{:S(2)}) collective-permute-start(bf16[64,2048]{1,0:T(8,128)(2,1)} %refs_0_.1), channel_id=1, source_target_pairs={{0,8},{4,12},{8,0},{12,4},{1,9},{5,13},{9,1},{13,5},{2,10},{6,14},... | collective-permute-start | bytes 786440 | tf_op jit(solution)/shard_map/ppermute | solution.py:156
  2.2 8.7 %collective-permute-start.1 = (bf16[64,2048]{1,0:T(8,128)(2,1)}, bf16[64,2048]{1,0:T(8,128)(2,1)S(1)}, u32[]{:S(2)}, u32[]{:S(2)}) collective-permute-start(bf16[64,2048]{1,0:T(8,128)(2,1)} %refs_0_.1), channel_id=1, source_target_pairs={{0,4},{4,0},{8,12},{12,8},{1,5},{5,1},{9,13},{13,9},{2,6},{6,2},{1... | collective-permute-start | bytes 786440 | tf_op jit(solution)/shard_map/ppermute | solution.py:156
  4.3 21.4 %collective-permute-start.5 = (bf16[64,3584]{1,0:T(8,128)(2,1)}, bf16[64,3584]{1,0:T(8,128)(2,1)S(1)}, u32[]{:S(2)}, u32[]{:S(2)}) collective-permute-start(bf16[64,3584]{1,0:T(8,128)(2,1)} %get-tuple-element.42), channel_id=1, source_target_pairs={{0,1},{1,0},{2,3},{3,2},{4,5},{5,4},{6,7},{7,6},{8,9},{9,8},{10,11... | collective-permute-start | bytes 1376264 | tf_op jit(solution)/shard_map/ppermute | solution.py:232
  4.8 21.0 %collective-permute-start.4 = (bf16[64,3584]{1,0:T(8,128)(2,1)}, bf16[64,3584]{1,0:T(8,128)(2,1)S(1)}, u32[]{:S(2)}, u32[]{:S(2)}) collective-permute-start(bf16[64,3584]{1,0:T(8,128)(2,1)} %get-tuple-element.42), channel_id=1, source_target_pairs={{1,2},{2,1},{5,6},{6,5},{9,10},{10,9},{13,14},{14,13},{17,18},{18,... | collective-permute-start | bytes 1376264 | tf_op jit(solution)/shard_map/ppermute | solution.py:232
  9.4 25.6 %collective-permute-start.12 = (bf16[64,3584]{1,0:T(8,128)(2,1)}, bf16[64,3584]{1,0:T(8,128)(2,1)S(1)}, u32[]{:S(2)}, u32[]{:S(2)}) collective-permute-start(bf16[64,3584]{1,0:T(8,128)(2,1)} %get-tuple-element.43), channel_id=1, source_target_pairs={{0,1},{1,0},{2,3},{3,2},{4,5},{5,4},{6,7},{7,6},{8,9},{9,8},{10,11... | collective-permute-start | bytes 1376264 | tf_op jit(solution)/shard_map/ppermute | solution.py:232
  10.2 3.5 %collective-permute-start.2 = (bf16[64,2048]{1,0:T(8,128)(2,1)S(1)}, bf16[64,2048]{1,0:T(8,128)(2,1)S(1)}, u32[]{:S(2)}, u32[]{:S(2)}) collective-permute-start(bf16[64,2048]{1,0:T(8,128)(2,1)S(1)} %collective-permute-done.refs_1_), channel_id=1, source_target_pairs={{0,4},{4,0},{8,12},{12,8},{1,5},{5,1},{9,13},{13,9},{2,6},{6,2},{1... | collective-permute-start | bytes 786440 | tf_op jit(solution)/shard_map/ppermute | solution.py:156
  10.9 0.7 copy-start.14
  11.6 23.4 %collective-permute-start.3 = (bf16[64,3584]{1,0:T(8,128)(2,1)}, bf16[64,3584]{1,0:T(8,128)(2,1)S(1)}, u32[]{:S(2)}, u32[]{:S(2)}) collective-permute-start(bf16[64,3584]{1,0:T(8,128)(2,1)} %get-tuple-element.43), channel_id=1, source_target_pairs={{1,2},{2,1},{5,6},{6,5},{9,10},{10,9},{13,14},{14,13},{17,18},{18,... | collective-permute-start | bytes 1376264 | tf_op jit(solution)/shard_map/ppermute | solution.py:232
  13.7 6.0 %copy-start = (bf16[1,1,537,128,128]{4,3,2,1,0:T(8,128)(2,1)S(1)}, bf16[1,1,537,128,128]{4,3,2,1,0:T(8,128)(2,1)}, u32[]{:S(2)}) copy-start(bf16[1,1,537,128,128]{4,3,2,1,0:T(8,128)(2,1)} %param.7) | copy-start | bytes 52789252
  19.7 0.9 copy-start.15
  20.7 9.3 %copy-start.1 = (bf16[1,1,537,128,128]{4,3,2,1,0:T(8,128)(2,1)S(1)}, bf16[1,1,537,128,128]{4,3,2,1,0:T(8,128)(2,1)}, u32[]{:S(2)}) copy-start(bf16[1,1,537,128,128]{4,3,2,1,0:T(8,128)(2,1)} %param.7) | copy-start | bytes 52789252
  25.8 9.2 %copy-start.9 = (bf16[64,3584]{1,0:T(8,128)(2,1)}, bf16[64,3584]{1,0:T(8,128)(2,1)S(1)}, u32[]{:S(2)}) copy-start(bf16[64,3584]{1,0:T(8,128)(2,1)S(1)} %collective-permute-done.5.refs_0_) | copy-start | bytes 1376260
  25.8 9.2 %copy-start.11 = (bf16[64,3584]{1,0:T(8,128)(2,1)}, bf16[64,3584]{1,0:T(8,128)(2,1)S(1)}, u32[]{:S(2)}) copy-start(bf16[64,3584]{1,0:T(8,128)(2,1)S(1)} %collective-permute-done.4.refs_3_) | copy-start | bytes 1376260
  26.2 15.2 %collective-permute-start.10 = (bf16[64,3584]{1,0:T(8,128)(2,1)S(1)}, bf16[64,3584]{1,0:T(8,128)(2,1)S(1)}, u32[]{:S(2)}, u32[]{:S(2)}) collective-permute-start(bf16[64,3584]{1,0:T(8,128)(2,1)S(1)} %get-tuple-element.40), channel_id=1, source_target_pairs={{1,2},{2,1},{5,6},{6,5},{9,10},{10,9},{13,14},{14,13},{17,18},{18,... | collective-permute-start | bytes 1376264 | tf_op jit(solution)/shard_map/ppermute | solution.py:232
  29.9 13.5 %collective-permute-start.8 = (bf16[64,3584]{1,0:T(8,128)(2,1)S(1)}, bf16[64,3584]{1,0:T(8,128)(2,1)S(1)}, u32[]{:S(2)}, u32[]{:S(2)}) collective-permute-start(bf16[64,3584]{1,0:T(8,128)(2,1)S(1)} %get-tuple-element.41), channel_id=1, source_target_pairs={{0,1},{1,0},{2,3},{3,2},{4,5},{5,4},{6,7},{7,6},{8,9},{9,8},{10,11... | collective-permute-start | bytes 1376264 | tf_op jit(solution)/shard_map/ppermute | solution.py:232
  35.4 15.9 %collective-permute-start.13 = (bf16[64,3584]{1,0:T(8,128)(2,1)S(1)}, bf16[64,3584]{1,0:T(8,128)(2,1)S(1)}, u32[]{:S(2)}, u32[]{:S(2)}) collective-permute-start(bf16[64,3584]{1,0:T(8,128)(2,1)S(1)} %get-tuple-element.36), channel_id=1, source_target_pairs={{1,2},{2,1},{5,6},{6,5},{9,10},{10,9},{13,14},{14,13},{17,18},{18,... | collective-permute-start | bytes 1376264 | tf_op jit(solution)/shard_map/ppermute | solution.py:232
  37.5 15.7 %collective-permute-start.6 = (bf16[64,3584]{1,0:T(8,128)(2,1)S(1)}, bf16[64,3584]{1,0:T(8,128)(2,1)S(1)}, u32[]{:S(2)}, u32[]{:S(2)}) collective-permute-start(bf16[64,3584]{1,0:T(8,128)(2,1)S(1)} %get-tuple-element.37), channel_id=1, source_target_pairs={{0,1},{1,0},{2,3},{3,2},{4,5},{5,4},{6,7},{7,6},{8,9},{9,8},{10,11... | collective-permute-start | bytes 1376264 | tf_op jit(solution)/shard_map/ppermute | solution.py:232
  43.7 19.3 %collective-permute-start.11 = (bf16[64,3584]{1,0:T(8,128)(2,1)S(1)}, bf16[64,3584]{1,0:T(8,128)(2,1)S(1)}, u32[]{:S(2)}, u32[]{:S(2)}) collective-permute-start(bf16[64,3584]{1,0:T(8,128)(2,1)S(1)} %get-tuple-element.38), channel_id=1, source_target_pairs={{0,1},{1,0},{2,3},{3,2},{4,5},{5,4},{6,7},{7,6},{8,9},{9,8},{10,11... | collective-permute-start | bytes 1376264 | tf_op jit(solution)/shard_map/ppermute | solution.py:232
  43.8 19.3 %collective-permute-start.9 = (bf16[64,3584]{1,0:T(8,128)(2,1)S(1)}, bf16[64,3584]{1,0:T(8,128)(2,1)S(1)}, u32[]{:S(2)}, u32[]{:S(2)}) collective-permute-start(bf16[64,3584]{1,0:T(8,128)(2,1)S(1)} %get-tuple-element.39), channel_id=1, source_target_pairs={{1,2},{2,1},{5,6},{6,5},{9,10},{10,9},{13,14},{14,13},{17,18},{18,... | collective-permute-start | bytes 1376264 | tf_op jit(solution)/shard_map/ppermute | solution.py:232
  53.2 0.8 copy-start.3
  53.5 22.6 %collective-permute-start.14 = (bf16[64,3584]{1,0:T(8,128)(2,1)S(1)}, bf16[64,3584]{1,0:T(8,128)(2,1)S(1)}, u32[]{:S(2)}, u32[]{:S(2)}) collective-permute-start(bf16[64,3584]{1,0:T(8,128)(2,1)S(1)} %get-tuple-element.34), channel_id=1, source_target_pairs={{0,1},{1,0},{2,3},{3,2},{4,5},{5,4},{6,7},{7,6},{8,9},{9,8},{10,11... | collective-permute-start | bytes 1376264 | tf_op jit(solution)/shard_map/ppermute | solution.py:232
  53.9 10.3 %copy-start.2 = (bf16[64,7168]{1,0:T(8,128)(2,1)S(1)}, bf16[64,7168]{1,0:T(8,128)(2,1)}, u32[]{:S(2)}) copy-start(bf16[64,7168]{1,0:T(8,128)(2,1)} %own.3) | copy-start | bytes 2752516
  53.9 10.3 %copy-start.10 = (bf16[64,3584]{1,0:T(8,128)(2,1)S(1)}, bf16[64,3584]{1,0:T(8,128)(2,1)}, u32[]{:S(2)}) copy-start(bf16[64,3584]{1,0:T(8,128)(2,1)} %copy-done.9) | copy-start | bytes 1376260
  53.9 10.3 %copy-start.12 = (bf16[64,3584]{1,0:T(8,128)(2,1)S(1)}, bf16[64,3584]{1,0:T(8,128)(2,1)}, u32[]{:S(2)}) copy-start(bf16[64,3584]{1,0:T(8,128)(2,1)} %copy-done.11) | copy-start | bytes 1376260
  54.0 22.1 %collective-permute-start.7 = (bf16[64,3584]{1,0:T(8,128)(2,1)S(1)}, bf16[64,3584]{1,0:T(8,128)(2,1)S(1)}, u32[]{:S(2)}, u32[]{:S(2)}) collective-permute-start(bf16[64,3584]{1,0:T(8,128)(2,1)S(1)} %get-tuple-element.35), channel_id=1, source_target_pairs={{1,2},{2,1},{5,6},{6,5},{9,10},{10,9},{13,14},{14,13},{17,18},{18,... | collective-permute-start | bytes 1376264 | tf_op jit(solution)/shard_map/ppermute | solution.py:232
  76.1 1.4 %copy-start.5 = (bf16[64,3584]{1,0:T(8,128)(2,1)}, bf16[64,3584]{1,0:T(8,128)(2,1)S(1)}, u32[]{:S(2)}) copy-start(bf16[64,3584]{1,0:T(8,128)(2,1)S(1)} %collective-permute-done.14.refs_2_) | copy-start | bytes 1376260
  76.1 1.4 %copy-start.7 = (bf16[64,3584]{1,0:T(8,128)(2,1)}, bf16[64,3584]{1,0:T(8,128)(2,1)S(1)}, u32[]{:S(2)}) copy-start(bf16[64,3584]{1,0:T(8,128)(2,1)S(1)} %collective-permute-done.7.refs_5_) | copy-start | bytes 1376260
  77.5 17.1 %collective-permute-start.17 = (bf16[64,3584]{1,0:T(8,128)(2,1)}, bf16[64,3584]{1,0:T(8,128)(2,1)}, u32[]{:S(2)}, u32[]{:S(2)}) collective-permute-start(bf16[64,3584]{1,0:T(8,128)(2,1)} %get-tuple-element.33), channel_id=1, source_target_pairs={{0,1},{1,0},{2,3},{3,2},{4,5},{5,4},{6,7},{7,6},{8,9},{9,8},{10,11... | collective-permute-start | bytes 1376264 | tf_op jit(solution)/shard_map/ppermute | solution.py:232
  77.5 17.1 %collective-permute-start.18 = (bf16[64,3584]{1,0:T(8,128)(2,1)}, bf16[64,3584]{1,0:T(8,128)(2,1)}, u32[]{:S(2)}, u32[]{:S(2)}) collective-permute-start(bf16[64,3584]{1,0:T(8,128)(2,1)} %get-tuple-element.31), channel_id=1, source_target_pairs={{1,2},{2,1},{5,6},{6,5},{9,10},{10,9},{13,14},{14,13},{17,18},{18,... | collective-permute-start | bytes 1376264 | tf_op jit(solution)/shard_map/ppermute | solution.py:232
  79.4 16.6 %collective-permute-start.15 = (bf16[64,3584]{1,0:T(8,128)(2,1)}, bf16[64,3584]{1,0:T(8,128)(2,1)S(1)}, u32[]{:S(2)}, u32[]{:S(2)}) collective-permute-start(bf16[64,3584]{1,0:T(8,128)(2,1)} %get-tuple-element.30), channel_id=1, source_target_pairs={{0,1},{1,0},{2,3},{3,2},{4,5},{5,4},{6,7},{7,6},{8,9},{9,8},{10,11... | collective-permute-start | bytes 1376264 | tf_op jit(solution)/shard_map/ppermute | solution.py:232
  80.9 17.4 %collective-permute-start.16 = (bf16[64,3584]{1,0:T(8,128)(2,1)}, bf16[64,3584]{1,0:T(8,128)(2,1)S(1)}, u32[]{:S(2)}, u32[]{:S(2)}) collective-permute-start(bf16[64,3584]{1,0:T(8,128)(2,1)} %get-tuple-element.29), channel_id=1, source_target_pairs={{1,2},{2,1},{5,6},{6,5},{9,10},{10,9},{13,14},{14,13},{17,18},{18,... | collective-permute-start | bytes 1376264 | tf_op jit(solution)/shard_map/ppermute | solution.py:232
  83.4 1.0 %copy-start.4 = (bf16[64,3584]{1,0:T(8,128)(2,1)S(1)}, bf16[64,3584]{1,0:T(8,128)(2,1)}, u32[]{:S(2)}) copy-start(bf16[64,3584]{1,0:T(8,128)(2,1)} %copy-done.3) | copy-start | bytes 1376260
  84.4 1.0 %copy-start.6 = (bf16[64,3584]{1,0:T(8,128)(2,1)S(1)}, bf16[64,3584]{1,0:T(8,128)(2,1)}, u32[]{:S(2)}) copy-start(bf16[64,3584]{1,0:T(8,128)(2,1)} %copy-done.5) | copy-start | bytes 1376260
  85.5 1.0 %copy-start.8 = (bf16[64,3584]{1,0:T(8,128)(2,1)S(1)}, bf16[64,3584]{1,0:T(8,128)(2,1)}, u32[]{:S(2)}) copy-start(bf16[64,3584]{1,0:T(8,128)(2,1)} %copy-done.7) | copy-start | bytes 1376260
  86.5 8.1 %copy-start.17 = (bf16[64,3584]{1,0:T(8,128)(2,1)S(1)}, bf16[64,3584]{1,0:T(8,128)(2,1)}, u32[]{:S(2)}) copy-start(bf16[64,3584]{1,0:T(8,128)(2,1)} %get-tuple-element.26) | copy-start | bytes 1376260
  94.6 3.7 %copy-start.16 = (bf16[64,3584]{1,0:T(8,128)(2,1)S(1)}, bf16[64,3584]{1,0:T(8,128)(2,1)}, u32[]{:S(2)}) copy-start(bf16[64,3584]{1,0:T(8,128)(2,1)} %get-tuple-element.25) | copy-start | bytes 1376260

commit v2 on v1

--- a/solution.py
+++ b/solution.py
@@ -36,11 +36,16 @@
 
 
 def first_partial_kernel(tile, masks, slot_of, me, *refs):
-    pieces, (blocks, out, grads) = refs[: len(masks)], refs[len(masks) :]
+    pieces, (blocks, out, grads, sems) = refs[: len(masks)], refs[len(masks) :]
     rows = pieces[0].shape[0]
-    for mask, piece in zip(masks, pieces):
+    copies = []
+    for i, (mask, piece) in enumerate(zip(masks, pieces)):
         at = pl.multiple_of((me[0] ^ mask) * rows, rows)
-        grads[pl.ds(at, rows), :] = piece[...]
+        copies.append(pltpu.make_async_copy(piece, grads.at[pl.ds(at, rows), :], sems.at[i]))
+    for copy in copies:
+        copy.start()
+    for copy in copies:
+        copy.wait()
     partial_body(0, tile, slot_of, grads, blocks, out)
 
 
@@ -51,9 +56,7 @@
 def weight_grad_kernel(chunk, tile, n, slot_of, where, count, own, grads, *refs):
     flows = refs[: n - 1], refs[n - 1 : 2 * n - 2]
     refs = refs[2 * n - 2 :]
-    if chunk:
-        refs = refs[1:]
-    out, done, acts, dense, zero, act_sem, sem = refs
+    out, done, acts, dense, zero, act_sem, sem = refs[-7:]
     me = where[0]
     rows, cols = dense.shape[0], dense.shape[1]
     part, width = acts.shape[0] // n, acts.shape[1]
@@ -77,11 +80,16 @@
         if method == "start" and chunk == 0:
             zero[...] = jnp.zeros_like(zero)
 
-            def clear(slot, carry):
-                pltpu.make_async_copy(zero, out.at[slot], sem).start()
-                return carry
-
-            lax.fori_loop(count[0], out.shape[0], clear, 0)
+            group = zero.shape[0]
+            groups = (out.shape[0] - count[0]) // group
+
+            @pl.loop(0, groups)
+            def _(i):
+                pltpu.make_async_copy(zero, out.at[pl.ds(count[0] + i * group, group)], sem).start()
+
+            @pl.loop(count[0] + groups * group, out.shape[0])
+            def _(slot):
+                pltpu.make_async_copy(zero.at[0], out.at[slot], sem).start()
 
     wide = min(512, grads.shape[1])
 
@@ -162,8 +170,9 @@
     sums, grads = pl.pallas_call(
         functools.partial(first_partial_kernel, tile, masks),
         out_shape=[jax.ShapeDtypeStruct((tokens, width), kind), jax.ShapeDtypeStruct((tokens, depth), kind)],
-        in_specs=[SMEM, SMEM] + [VMEM] * (R + 1),
+        in_specs=[SMEM, SMEM] + [ANY] * R + [VMEM],
         out_specs=[VMEM, VMEM],
+        scratch_shapes=[pltpu.SemaphoreType.DMA((R,))],
         compiler_params=params(16),
         cost_estimate=work,
         name="partial0",
@@ -186,10 +195,11 @@
     def rows_of(h, d):
         return lax.dynamic_slice_in_dim(partial[h], jnp.clip(d, 0, n - 1) * part, part, 0)
 
-    def weight_grad(h, slot_of, out):
+    def weight_grad(h, messages, out):
         flows = [came[h][e][j] for e in range(2) for j in range(n - 1)]
         given = [slot_of, c[None].astype(jnp.int32), count, activations, grads, *flows]
-        specs = [SMEM, SMEM, SMEM, ANY, VMEM] + [ANY] * (2 * n - 2)
+        given += messages
+        specs = [SMEM, SMEM, SMEM, ANY, VMEM] + [ANY] * (2 * n - 2 + len(messages))
         if h:
             given.append(out)
             specs.append(ANY)
@@ -201,7 +211,7 @@
             scratch_shapes=[
                 pltpu.VMEM((tokens, width), kind),
                 pltpu.VMEM((row_blocks // CHUNKS, col_blocks, BLOCK, BLOCK), kind),
-                pltpu.VMEM((BLOCK, BLOCK), kind),
+                pltpu.VMEM((8, BLOCK, BLOCK), kind),
                 pltpu.SemaphoreType.DMA,
                 pltpu.SemaphoreType.DMA,
             ],
@@ -234,7 +244,7 @@
             if k == 1 and h + 1 < CHUNKS:
                 add_partial(h + 1, after)
             if k == n - 1:
-                out, done = weight_grad(h, after, out)
+                out, done = weight_grad(h, messages, out)
 
     hidden_parts = []
     inner = (c > 0) & (c < n - 1)

time: 101 us -> 91.3 us (0.904)
  local copies, waits for them, and re-layouts: 13.2 us -> 7.23 us
  starting transfers between devices: 25.8 us -> 29.1 us
  other arithmetic: 7.15 us -> 3.98 us
  waiting for transfers between devices: 21.6 us -> 19.4 us
  Pallas kernels: 29.9 us -> 28.3 us
    unnamed x38 -> x10, local copies, waits for them, and re-layouts: 11.1 us -> 6.02 us
    ppermute x16, starting transfers between devices: 24.2 us -> 27.5 us  [shards(): came[h][e].append(lax.ppermute(messages[e], 'col', pairs))]
    ppermute x16, waiting for transfers between devices: 21.6 us -> 19.3 us  [shards(): came[h][e].append(lax.ppermute(messages[e], 'col', pairs))]
    pallas_call x2, Pallas kernels: 19.8 us -> 18.2 us  [weight_grad(): pl.pallas_call(functools.partial(weight_grad_kernel, h, tile, n), out_sha...]
    convert_element_type x2, other arithmetic: 1.64 us -> 0.4 us  [shards(): hidden_parts.append(total.astype(kind))]
  transfers between devices with their start and end apart: 19 -> 19, of which waited for: 6 -> 4; matrix products, arithmetic and copies ran while one was open for 7% -> 4% of each run, Pallas kernels for 30% -> 32%
where the time goes in v2:
time: 91.3 us; the launch traced here: 89.6 us
  starting transfers between devices  29.1 us (32%)
  Pallas kernels  28.3 us (31%)
  waiting for transfers between devices  19.4 us (21%)
  local copies, waits for them, and re-layouts  7.23 us (8%)
  other arithmetic  3.98 us (4%)
  between operations  1.66 us (2%)
    ppermute x16, starting transfers between devices, shards(): came[h][e].append(lax.ppermute(messages[e], 'col', pairs))  27.5 us
    ppermute x16, waiting for transfers between devices, shards(): came[h][e].append(lax.ppermute(messages[e], 'col', pairs))  19.3 us
    pallas_call x2, Pallas kernels, weight_grad(): pl.pallas_call(functools.partial(weight_grad_kernel, h, tile, n), out_sha...  18.2 us
    unnamed x10, local copies, waits for them, and re-layouts  6.02 us
    pallas_call x1, Pallas kernels, shards(): pl.pallas_call(functools.partial(first_partial_kernel, tile, masks), out_...  5.13 us
    pallas_call x1, Pallas kernels, add_partial(): pl.pallas_call(functools.partial(partial_kernel, h, tile), out_shape=jax....  5 us
  transfers between devices with their start and end apart: 19, of which 4 were waited for; matrix products, arithmetic and copies ran while one was open for 4% of the time, Pallas kernels for 32%

profile of v2, /device:TPU:12, one launch (start us, length us, event | category | flops | bytes accessed | tf_op | source)
XLA Modules:
  0.0 89.6 jit_solution(9965133878435006748)
XLA Ops:
  0.6 0.0 copy-start.3
  0.6 0.0 copy-start.4
  0.6 1.6 %collective-permute-start = (bf16[64,2048]{1,0:T(8,128)(2,1)}, bf16[64,2048]{1,0:T(8,128)(2,1)S(1)}, u32[]{:S(2)}, u32[]{:S(2)}) collective-permute-start(bf16[64,2048]{1,0:T(8,128)(2,1)} %refs_0_.1), channel_id=1, source_target_pairs={{0,8},{4,12},{8,0},{12,4},{1,9},{5,13},{9,1},{13,5},{2,10},{6,14},... | collective-permute-start | bytes 786440 | tf_op jit(solution)/shard_map/ppermute | solution.py:164
  2.2 0.0 collective-permute-start.1
  2.2 1.2 %fusion.1 = (bf16[64,3584]{1,0:T(8,128)(2,1)S(1)}, bf16[64,3584]{1,0:T(8,128)(2,1)S(1)}) fusion(bf16[64,7168]{1,0:T(8,128)(2,1)} %own.3), kind=kLoop, calls=%fused_computation.21 | loop fusion | bytes 1835008 | tf_op jit(solution)/shard_map/slice | solution.py:231
  3.4 3.5 %collective-permute-start.5 = (bf16[64,3584]{1,0:T(8,128)(2,1)S(1)}, bf16[64,3584]{1,0:T(8,128)(2,1)S(1)}, u32[]{:S(2)}, u32[]{:S(2)}) collective-permute-start(bf16[64,3584]{1,0:T(8,128)(2,1)S(1)} %get-tuple-element.38), channel_id=1, source_target_pairs={{1,2},{2,1},{5,6},{6,5},{9,10},{10,9},{13,14},{14,13},{17,18},{18,... | collective-permute-start | bytes 1376264 | tf_op jit(solution)/shard_map/ppermute | solution.py:242
  6.9 0.1 collective-permute-start.6
  7.0 2.0 %collective-permute-start.3 = (bf16[64,3584]{1,0:T(8,128)(2,1)S(1)}, bf16[64,3584]{1,0:T(8,128)(2,1)S(1)}, u32[]{:S(2)}, u32[]{:S(2)}) collective-permute-start(bf16[64,3584]{1,0:T(8,128)(2,1)S(1)} %get-tuple-element.39), channel_id=1, source_target_pairs={{0,1},{1,0},{2,3},{3,2},{4,5},{5,4},{6,7},{7,6},{8,9},{9,8},{10,11... | collective-permute-start | bytes 1376264 | tf_op jit(solution)/shard_map/ppermute | solution.py:242
  9.7 0.0 copy-done.4
  9.7 0.0 collective-permute-done.refs_1_
  9.7 0.1 collective-permute-start.2
  9.8 0.5 select_reduce_fusion.slot_of
  10.3 0.0 collective-permute-done.1.refs_2_
  10.4 2.7 %collective-permute-start.4 = (bf16[64,3584]{1,0:T(8,128)(2,1)S(1)}, bf16[64,3584]{1,0:T(8,128)(2,1)S(1)}, u32[]{:S(2)}, u32[]{:S(2)}) collective-permute-start(bf16[64,3584]{1,0:T(8,128)(2,1)S(1)} %get-tuple-element.39), channel_id=1, source_target_pairs={{1,2},{2,1},{5,6},{6,5},{9,10},{10,9},{13,14},{14,13},{17,18},{18,... | collective-permute-start | bytes 1376264 | tf_op jit(solution)/shard_map/ppermute | solution.py:242
  13.0 0.0 collective-permute-done.2.refs_3_
  13.0 0.0 copy-done.3
  13.0 0.0 copy-start
  13.1 6.0 %copy-done = bf16[1,1,537,128,128]{4,3,2,1,0:T(8,128)(2,1)S(1)} copy-done((bf16[1,1,537,128,128]{4,3,2,1,0:T(8,128)(2,1)S(1)}, bf16[1,1,537,128,128]{4,3,2,1,0:T(8,128)(2,1)}, u32[]{:S(2)}) %copy-start) | copy-done | bytes 17596440
  19.0 0.0 copy-start.1
  19.0 5.1 %partial0.1 = (bf16[256,3584]{1,0:T(8,128)(2,1)S(1)}, bf16[256,2048]{1,0:T(8,128)(2,1)S(1)}) custom-call(s32[896]{0:T(1024)S(1)} %select_reduce_fusion.slot_of, s32[1]{0:T(128)} %bitcast.1.me, bf16[64,2048]{1,0:T(8,128)(2,1)S(1)} %copy-done.3, bf16[64,2048]{1,0:T(8,128)(2,1)S(1)} %collective-permute-done.refs_1_, ...), custom_call_target="tpu_custom_call" | custom-call | flops 3758096384 | bytes 14680064 | tf_op jit(solution)/shard_map/partial0/pallas_call | solution.py:170
  24.2 0.0 collective-permute-done.5.refs_3_
  24.2 0.0 collective-permute-done.6.refs_0_
  24.2 0.4 add_select_fusion.10
  24.6 0.1 collective-permute-start.11
  24.6 3.2 %collective-permute-start.12 = (bf16[64,3584]{1,0:T(8,128)(2,1)S(1)}, bf16[64,3584]{1,0:T(8,128)(2,1)S(1)}, u32[]{:S(2)}, u32[]{:S(2)}) collective-permute-start(bf16[64,3584]{1,0:T(8,128)(2,1)S(1)} %get-tuple-element.36), channel_id=1, source_target_pairs={{1,2},{2,1},{5,6},{6,5},{9,10},{10,9},{13,14},{14,13},{17,18},{18,... | collective-permute-start | bytes 1376264 | tf_op jit(solution)/shard_map/ppermute | solution.py:242
  27.8 0.0 copy-done.1
  27.9 5.0 %partial1.1 = bf16[256,3584]{1,0:T(8,128)(2,1)S(1)} custom-call(s32[896]{0:T(1024)S(1)} %select_reduce_fusion.slot_of, bf16[256,2048]{1,0:T(8,128)(2,1)S(1)} %get-tuple-element.14.grads, bf16[537,128,128]{2,1,0:T(8,128)(2,1)S(1)} %bitcast.10), custom_call_target="tpu_custom_call" | custom-call | flops 3758096384 | bytes 14680064 | tf_op jit(solution)/shard_map/partial1/pallas_call | solution.py:184
  32.9 0.0 collective-permute-done.3.refs_0_
  32.9 0.0 collective-permute-done.4.refs_3_
  32.9 0.3 add_select_fusion.8
  33.2 0.1 collective-permute-start.7
  33.3 2.7 %collective-permute-start.8 = (bf16[64,3584]{1,0:T(8,128)(2,1)S(1)}, bf16[64,3584]{1,0:T(8,128)(2,1)S(1)}, u32[]{:S(2)}, u32[]{:S(2)}) collective-permute-start(bf16[64,3584]{1,0:T(8,128)(2,1)S(1)} %get-tuple-element.32), channel_id=1, source_target_pairs={{1,2},{2,1},{5,6},{6,5},{9,10},{10,9},{13,14},{14,13},{17,18},{18,... | collective-permute-start | bytes 1376264 | tf_op jit(solution)/shard_map/ppermute | solution.py:242
  36.0 4.0 %collective-permute-done.11.refs_1_ = bf16[64,3584]{1,0:T(8,128)(2,1)S(1)} collective-permute-done((bf16[64,3584]{1,0:T(8,128)(2,1)S(1)}, bf16[64,3584]{1,0:T(8,128)(2,1)S(1)}, u32[]{:S(2)}, u32[]{:S(2)}) %collective-permute-start.11) | collective-permute-done | bytes 458784 | tf_op jit(solution)/shard_map/ppermute | solution.py:242
  40.0 0.0 collective-permute-done.12.refs_4_
  40.0 0.3 add_select_fusion.4
  40.3 0.1 collective-permute-start.13
  40.4 3.1 %collective-permute-start.14 = (bf16[64,3584]{1,0:T(8,128)(2,1)S(1)}, bf16[64,3584]{1,0:T(8,128)(2,1)S(1)}, u32[]{:S(2)}, u32[]{:S(2)}) collective-permute-start(bf16[64,3584]{1,0:T(8,128)(2,1)S(1)} %get-tuple-element.34), channel_id=1, source_target_pairs={{1,2},{2,1},{5,6},{6,5},{9,10},{10,9},{13,14},{14,13},{17,18},{18,... | collective-permute-start | bytes 1376264 | tf_op jit(solution)/shard_map/ppermute | solution.py:242
  43.5 6.3 %collective-permute-done.7.refs_1_ = bf16[64,3584]{1,0:T(8,128)(2,1)S(1)} collective-permute-done((bf16[64,3584]{1,0:T(8,128)(2,1)S(1)}, bf16[64,3584]{1,0:T(8,128)(2,1)S(1)}, u32[]{:S(2)}, u32[]{:S(2)}) %collective-permute-start.7) | collective-permute-done | bytes 458784 | tf_op jit(solution)/shard_map/ppermute | solution.py:242
  49.8 0.0 collective-permute-done.8.refs_4_
  49.8 0.3 add_select_fusion.7
  50.2 3.1 %collective-permute-start.10 = (bf16[64,3584]{1,0:T(8,128)(2,1)S(1)}, bf16[64,3584]{1,0:T(8,128)(2,1)S(1)}, u32[]{:S(2)}, u32[]{:S(2)}) collective-permute-start(bf16[64,3584]{1,0:T(8,128)(2,1)S(1)} %get-tuple-element.31), channel_id=1, source_target_pairs={{1,2},{2,1},{5,6},{6,5},{9,10},{10,9},{13,14},{14,13},{17,18},{18,... | collective-permute-start | bytes 1376264 | tf_op jit(solution)/shard_map/ppermute | solution.py:242
  53.3 0.0 copy-start.2
  53.3 0.1 collective-permute-start.9
  53.4 6.3 %collective-permute-done.13.refs_2_ = bf16[64,3584]{1,0:T(8,128)(2,1)S(1)} collective-permute-done((bf16[64,3584]{1,0:T(8,128)(2,1)S(1)}, bf16[64,3584]{1,0:T(8,128)(2,1)S(1)}, u32[]{:S(2)}, u32[]{:S(2)}) %collective-permute-start.13) | collective-permute-done | bytes 458784 | tf_op jit(solution)/shard_map/ppermute | solution.py:242
  59.7 0.0 collective-permute-done.14.refs_5_
  59.7 0.3 constant_dynamic-slice_fusion.1
  60.0 0.1 collective-permute-start.15
  60.1 3.1 %collective-permute-start.16 = (bf16[64,3584]{1,0:T(8,128)(2,1)S(1)}, bf16[64,3584]{1,0:T(8,128)(2,1)S(1)}, u32[]{:S(2)}, u32[]{:S(2)}) collective-permute-start(bf16[64,3584]{1,0:T(8,128)(2,1)S(1)} %get-tuple-element.25.refs_7_), channel_id=1, source_target_pairs={{1,2},{2,1},{5,6},{6,5},{9,10},{10,9},{13,14},{14,13},{17,18},{18,... | collective-permute-start | bytes 1376264 | tf_op jit(solution)/shard_map/ppermute | solution.py:242
  63.2 0.0 copy-done.2
  63.2 8.8 %weight_grad0.1 = (bf16[537,128,128]{2,1,0:T(8,128)(2,1)}, s32[1]{0:T(128)}) custom-call(s32[896]{0:T(1024)S(1)} %select_reduce_fusion.slot_of, s32[1]{0:T(128)} %bitcast.3.where, s32[1]{0:T(128)} %bitcast.7.count, bf16[64,7168]{1,0:T(8,128)(2,1)S(1)} %copy-done.2, bf16[256,2048]{1,0:T(8,128)(2,1)S(1)} %get-tuple-element.14.grads, ...), custom_call_target="tpu_custom_call" | custom-call | flops 3758096384 | bytes 8798208 | tf_op jit(solution)/shard_map/weight_grad0/pallas_call | solution.py:206
  72.0 0.0 collective-permute-done.10.refs_5_
  72.0 0.0 collective-permute-done.9.refs_2_
  72.0 0.3 add_select_fusion
  72.4 0.3 collective-permute-start.17
  72.7 3.5 %collective-permute-start.18 = (bf16[64,3584]{1,0:T(8,128)(2,1)S(1)}, bf16[64,3584]{1,0:T(8,128)(2,1)S(1)}, u32[]{:S(2)}, u32[]{:S(2)}) collective-permute-start(bf16[64,3584]{1,0:T(8,128)(2,1)S(1)} %get-tuple-element.27.refs_7_), channel_id=1, source_target_pairs={{1,2},{2,1},{5,6},{6,5},{9,10},{10,9},{13,14},{14,13},{17,18},{18,... | collective-permute-start | bytes 1376264 | tf_op jit(solution)/shard_map/ppermute | solution.py:242
  76.2 9.3 %weight_grad1.1 = (bf16[537,128,128]{2,1,0:T(8,128)(2,1)}, s32[1]{0:T(128)}) custom-call(s32[896]{0:T(1024)S(1)} %select_reduce_fusion.slot_of, s32[1]{0:T(128)} %bitcast.3.where, s32[1]{0:T(128)} %bitcast.8.count, bf16[64,7168]{1,0:T(8,128)(2,1)S(1)} %copy-done.2, bf16[256,2048]{1,0:T(8,128)(2,1)S(1)} %get-tuple-element.14.grads, ...), custom_call_target="tpu_custom_call", output_to_operand_aliasing={{0}: (13, {})} | custom-call | flops 3758096384 | bytes 8798208 | tf_op jit(solution)/shard_map/weight_grad1/pallas_call | solution.py:206
  85.6 0.0 collective-permute-done.15
  85.6 0.0 collective-permute-done.16
  85.6 0.2 add_convert_fusion.1
  85.8 2.6 %collective-permute-done.17 = bf16[64,3584]{1,0:T(8,128)(2,1)S(1)} collective-permute-done((bf16[64,3584]{1,0:T(8,128)(2,1)S(1)}, bf16[64,3584]{1,0:T(8,128)(2,1)S(1)}, u32[]{:S(2)}, u32[]{:S(2)}) %collective-permute-start.17) | collective-permute-done | bytes 458784 | tf_op jit(solution)/shard_map/ppermute | solution.py:242
  88.5 0.0 collective-permute-done.18
  88.5 0.2 add_convert_fusion
  88.7 1.0 %pad_maximum_fusion = bf16[64,7168]{1,0:T(8,128)(2,1)} fusion(bf16[64,3584]{1,0:T(8,128)(2,1)S(1)} %add_convert_fusion, bf16[64,3584]{1,0:T(8,128)(2,1)S(1)} %add_convert_fusion.1), kind=kLoop, calls=%fused_computation.3 | loop fusion | flops 1835008 | bytes 1835008 | tf_op jit(solution)/shard_map/concatenate | solution.py:256
  (2 shorter events, 0.0 us)
Async XLA Ops:
  0.6 12.4 %copy-start.3 = (bf16[64,2048]{1,0:T(8,128)(2,1)S(1)}, bf16[64,2048]{1,0:T(8,128)(2,1)}, u32[]{:S(2)}) copy-start(bf16[64,2048]{1,0:T(8,128)(2,1)} %refs_0_.1) | copy-start | bytes 786436
  0.6 9.0 %copy-start.4 = (s32[1,1,537]{2,1,0:T(1,128)S(1)}, s32[1,1,537]{2,1,0:T(1,128)}, u32[]{:S(2)}) copy-start(s32[1,1,537]{2,1,0:T(1,128)} %param.8) | copy-start | bytes 6448
  0.6 9.1 %collective-permute-start = (bf16[64,2048]{1,0:T(8,128)(2,1)}, bf16[64,2048]{1,0:T(8,128)(2,1)S(1)}, u32[]{:S(2)}, u32[]{:S(2)}) collective-permute-start(bf16[64,2048]{1,0:T(8,128)(2,1)} %refs_0_.1), channel_id=1, source_target_pairs={{0,8},{4,12},{8,0},{12,4},{1,9},{5,13},{9,1},{13,5},{2,10},{6,14},... | collective-permute-start | bytes 786440 | tf_op jit(solution)/shard_map/ppermute | solution.py:164
  2.2 8.1 %collective-permute-start.1 = (bf16[64,2048]{1,0:T(8,128)(2,1)}, bf16[64,2048]{1,0:T(8,128)(2,1)S(1)}, u32[]{:S(2)}, u32[]{:S(2)}) collective-permute-start(bf16[64,2048]{1,0:T(8,128)(2,1)} %refs_0_.1), channel_id=1, source_target_pairs={{0,4},{4,0},{8,12},{12,8},{1,5},{5,1},{9,13},{13,9},{2,6},{6,2},{1... | collective-permute-start | bytes 786440 | tf_op jit(solution)/shard_map/ppermute | solution.py:164
  3.4 20.8 %collective-permute-start.5 = (bf16[64,3584]{1,0:T(8,128)(2,1)S(1)}, bf16[64,3584]{1,0:T(8,128)(2,1)S(1)}, u32[]{:S(2)}, u32[]{:S(2)}) collective-permute-start(bf16[64,3584]{1,0:T(8,128)(2,1)S(1)} %get-tuple-element.38), channel_id=1, source_target_pairs={{1,2},{2,1},{5,6},{6,5},{9,10},{10,9},{13,14},{14,13},{17,18},{18,... | collective-permute-start | bytes 1376264 | tf_op jit(solution)/shard_map/ppermute | solution.py:242
  6.9 17.3 %collective-permute-start.6 = (bf16[64,3584]{1,0:T(8,128)(2,1)S(1)}, bf16[64,3584]{1,0:T(8,128)(2,1)S(1)}, u32[]{:S(2)}, u32[]{:S(2)}) collective-permute-start(bf16[64,3584]{1,0:T(8,128)(2,1)S(1)} %get-tuple-element.38), channel_id=1, source_target_pairs={{0,1},{1,0},{2,3},{3,2},{4,5},{5,4},{6,7},{7,6},{8,9},{9,8},{10,11... | collective-permute-start | bytes 1376264 | tf_op jit(solution)/shard_map/ppermute | solution.py:242
  7.0 25.9 %collective-permute-start.3 = (bf16[64,3584]{1,0:T(8,128)(2,1)S(1)}, bf16[64,3584]{1,0:T(8,128)(2,1)S(1)}, u32[]{:S(2)}, u32[]{:S(2)}) collective-permute-start(bf16[64,3584]{1,0:T(8,128)(2,1)S(1)} %get-tuple-element.39), channel_id=1, source_target_pairs={{0,1},{1,0},{2,3},{3,2},{4,5},{5,4},{6,7},{7,6},{8,9},{9,8},{10,11... | collective-permute-start | bytes 1376264 | tf_op jit(solution)/shard_map/ppermute | solution.py:242
  9.7 3.3 %collective-permute-start.2 = (bf16[64,2048]{1,0:T(8,128)(2,1)S(1)}, bf16[64,2048]{1,0:T(8,128)(2,1)S(1)}, u32[]{:S(2)}, u32[]{:S(2)}) collective-permute-start(bf16[64,2048]{1,0:T(8,128)(2,1)S(1)} %collective-permute-done.refs_1_), channel_id=1, source_target_pairs={{0,4},{4,0},{8,12},{12,8},{1,5},{5,1},{9,13},{13,9},{2,6},{6,2},{1... | collective-permute-start | bytes 786440 | tf_op jit(solution)/shard_map/ppermute | solution.py:164
  10.4 22.5 %collective-permute-start.4 = (bf16[64,3584]{1,0:T(8,128)(2,1)S(1)}, bf16[64,3584]{1,0:T(8,128)(2,1)S(1)}, u32[]{:S(2)}, u32[]{:S(2)}) collective-permute-start(bf16[64,3584]{1,0:T(8,128)(2,1)S(1)} %get-tuple-element.39), channel_id=1, source_target_pairs={{1,2},{2,1},{5,6},{6,5},{9,10},{10,9},{13,14},{14,13},{17,18},{18,... | collective-permute-start | bytes 1376264 | tf_op jit(solution)/shard_map/ppermute | solution.py:242
  13.0 6.0 %copy-start = (bf16[1,1,537,128,128]{4,3,2,1,0:T(8,128)(2,1)S(1)}, bf16[1,1,537,128,128]{4,3,2,1,0:T(8,128)(2,1)}, u32[]{:S(2)}) copy-start(bf16[1,1,537,128,128]{4,3,2,1,0:T(8,128)(2,1)} %param.7) | copy-start | bytes 52789252
  19.0 8.8 %copy-start.1 = (bf16[1,1,537,128,128]{4,3,2,1,0:T(8,128)(2,1)S(1)}, bf16[1,1,537,128,128]{4,3,2,1,0:T(8,128)(2,1)}, u32[]{:S(2)}) copy-start(bf16[1,1,537,128,128]{4,3,2,1,0:T(8,128)(2,1)} %param.7) | copy-start | bytes 52789252
  24.6 15.4 %collective-permute-start.11 = (bf16[64,3584]{1,0:T(8,128)(2,1)S(1)}, bf16[64,3584]{1,0:T(8,128)(2,1)S(1)}, u32[]{:S(2)}, u32[]{:S(2)}) collective-permute-start(bf16[64,3584]{1,0:T(8,128)(2,1)S(1)} %get-tuple-element.37), channel_id=1, source_target_pairs={{0,1},{1,0},{2,3},{3,2},{4,5},{5,4},{6,7},{7,6},{8,9},{9,8},{10,11... | collective-permute-start | bytes 1376264 | tf_op jit(solution)/shard_map/ppermute | solution.py:242
  24.6 15.4 %collective-permute-start.12 = (bf16[64,3584]{1,0:T(8,128)(2,1)S(1)}, bf16[64,3584]{1,0:T(8,128)(2,1)S(1)}, u32[]{:S(2)}, u32[]{:S(2)}) collective-permute-start(bf16[64,3584]{1,0:T(8,128)(2,1)S(1)} %get-tuple-element.36), channel_id=1, source_target_pairs={{1,2},{2,1},{5,6},{6,5},{9,10},{10,9},{13,14},{14,13},{17,18},{18,... | collective-permute-start | bytes 1376264 | tf_op jit(solution)/shard_map/ppermute | solution.py:242
  33.2 16.6 %collective-permute-start.7 = (bf16[64,3584]{1,0:T(8,128)(2,1)S(1)}, bf16[64,3584]{1,0:T(8,128)(2,1)S(1)}, u32[]{:S(2)}, u32[]{:S(2)}) collective-permute-start(bf16[64,3584]{1,0:T(8,128)(2,1)S(1)} %get-tuple-element.33), channel_id=1, source_target_pairs={{0,1},{1,0},{2,3},{3,2},{4,5},{5,4},{6,7},{7,6},{8,9},{9,8},{10,11... | collective-permute-start | bytes 1376264 | tf_op jit(solution)/shard_map/ppermute | solution.py:242
  33.3 16.5 %collective-permute-start.8 = (bf16[64,3584]{1,0:T(8,128)(2,1)S(1)}, bf16[64,3584]{1,0:T(8,128)(2,1)S(1)}, u32[]{:S(2)}, u32[]{:S(2)}) collective-permute-start(bf16[64,3584]{1,0:T(8,128)(2,1)S(1)} %get-tuple-element.32), channel_id=1, source_target_pairs={{1,2},{2,1},{5,6},{6,5},{9,10},{10,9},{13,14},{14,13},{17,18},{18,... | collective-permute-start | bytes 1376264 | tf_op jit(solution)/shard_map/ppermute | solution.py:242
  40.3 19.3 %collective-permute-start.13 = (bf16[64,3584]{1,0:T(8,128)(2,1)S(1)}, bf16[64,3584]{1,0:T(8,128)(2,1)S(1)}, u32[]{:S(2)}, u32[]{:S(2)}) collective-permute-start(bf16[64,3584]{1,0:T(8,128)(2,1)S(1)} %get-tuple-element.35), channel_id=1, source_target_pairs={{0,1},{1,0},{2,3},{3,2},{4,5},{5,4},{6,7},{7,6},{8,9},{9,8},{10,11... | collective-permute-start | bytes 1376264 | tf_op jit(solution)/shard_map/ppermute | solution.py:242
  40.4 19.2 %collective-permute-start.14 = (bf16[64,3584]{1,0:T(8,128)(2,1)S(1)}, bf16[64,3584]{1,0:T(8,128)(2,1)S(1)}, u32[]{:S(2)}, u32[]{:S(2)}) collective-permute-start(bf16[64,3584]{1,0:T(8,128)(2,1)S(1)} %get-tuple-element.34), channel_id=1, source_target_pairs={{1,2},{2,1},{5,6},{6,5},{9,10},{10,9},{13,14},{14,13},{17,18},{18,... | collective-permute-start | bytes 1376264 | tf_op jit(solution)/shard_map/ppermute | solution.py:242
  50.2 21.9 %collective-permute-start.10 = (bf16[64,3584]{1,0:T(8,128)(2,1)S(1)}, bf16[64,3584]{1,0:T(8,128)(2,1)S(1)}, u32[]{:S(2)}, u32[]{:S(2)}) collective-permute-start(bf16[64,3584]{1,0:T(8,128)(2,1)S(1)} %get-tuple-element.31), channel_id=1, source_target_pairs={{1,2},{2,1},{5,6},{6,5},{9,10},{10,9},{13,14},{14,13},{17,18},{18,... | collective-permute-start | bytes 1376264 | tf_op jit(solution)/shard_map/ppermute | solution.py:242
  53.3 9.9 %copy-start.2 = (bf16[64,7168]{1,0:T(8,128)(2,1)S(1)}, bf16[64,7168]{1,0:T(8,128)(2,1)}, u32[]{:S(2)}) copy-start(bf16[64,7168]{1,0:T(8,128)(2,1)} %own.3) | copy-start | bytes 2752516
  53.3 18.8 %collective-permute-start.9 = (bf16[64,3584]{1,0:T(8,128)(2,1)S(1)}, bf16[64,3584]{1,0:T(8,128)(2,1)S(1)}, u32[]{:S(2)}, u32[]{:S(2)}) collective-permute-start(bf16[64,3584]{1,0:T(8,128)(2,1)S(1)} %get-tuple-element.30), channel_id=1, source_target_pairs={{0,1},{1,0},{2,3},{3,2},{4,5},{5,4},{6,7},{7,6},{8,9},{9,8},{10,11... | collective-permute-start | bytes 1376264 | tf_op jit(solution)/shard_map/ppermute | solution.py:242
  60.0 25.6 %collective-permute-start.15 = (bf16[64,3584]{1,0:T(8,128)(2,1)S(1)}, bf16[64,3584]{1,0:T(8,128)(2,1)S(1)}, u32[]{:S(2)}, u32[]{:S(2)}) collective-permute-start(bf16[64,3584]{1,0:T(8,128)(2,1)S(1)} %get-tuple-element.26.refs_6_), channel_id=1, source_target_pairs={{0,1},{1,0},{2,3},{3,2},{4,5},{5,4},{6,7},{7,6},{8,9},{9,8},{10,11... | collective-permute-start | bytes 1376264 | tf_op jit(solution)/shard_map/ppermute | solution.py:242
  60.1 25.5 %collective-permute-start.16 = (bf16[64,3584]{1,0:T(8,128)(2,1)S(1)}, bf16[64,3584]{1,0:T(8,128)(2,1)S(1)}, u32[]{:S(2)}, u32[]{:S(2)}) collective-permute-start(bf16[64,3584]{1,0:T(8,128)(2,1)S(1)} %get-tuple-element.25.refs_7_), channel_id=1, source_target_pairs={{1,2},{2,1},{5,6},{6,5},{9,10},{10,9},{13,14},{14,13},{17,18},{18,... | collective-permute-start | bytes 1376264 | tf_op jit(solution)/shard_map/ppermute | solution.py:242
  72.4 16.1 %collective-permute-start.17 = (bf16[64,3584]{1,0:T(8,128)(2,1)S(1)}, bf16[64,3584]{1,0:T(8,128)(2,1)S(1)}, u32[]{:S(2)}, u32[]{:S(2)}) collective-permute-start(bf16[64,3584]{1,0:T(8,128)(2,1)S(1)} %get-tuple-element.29.refs_6_), channel_id=1, source_target_pairs={{0,1},{1,0},{2,3},{3,2},{4,5},{5,4},{6,7},{7,6},{8,9},{9,8},{10,11... | collective-permute-start | bytes 1376264 | tf_op jit(solution)/shard_map/ppermute | solution.py:242
  72.7 15.7 %collective-permute-start.18 = (bf16[64,3584]{1,0:T(8,128)(2,1)S(1)}, bf16[64,3584]{1,0:T(8,128)(2,1)S(1)}, u32[]{:S(2)}, u32[]{:S(2)}) collective-permute-start(bf16[64,3584]{1,0:T(8,128)(2,1)S(1)} %get-tuple-element.27.refs_7_), channel_id=1, source_target_pairs={{1,2},{2,1},{5,6},{6,5},{9,10},{10,9},{13,14},{14,13},{17,18},{18,... | collective-permute-start | bytes 1376264 | tf_op jit(solution)/shard_map/ppermute | solution.py:242

commit v3 on v2

--- a/solution.py
+++ b/solution.py
@@ -77,7 +77,7 @@
                 getattr(copy, method)()
             else:
                 pl.when(needed)(getattr(copy, method))
-        if method == "start" and chunk == 0:
+        if method == "start" and chunk == CHUNKS - 1:
             zero[...] = jnp.zeros_like(zero)
 
             group = zero.shape[0]
@@ -115,7 +115,7 @@
         return live
 
     live = lax.fori_loop(0, rows * BLOCK // tile, step, jnp.int32(0))
-    if chunk == 0:
+    if chunk == CHUNKS - 1:
         live = live + out.shape[0] - count[0]
 
     def drain(i, carry):

time: 91.3 us -> 91.3 us (level)
  transfers between devices with their start and end apart: 19 -> 19, of which waited for: 4 -> 4; matrix products, arithmetic and copies ran while one was open for 4% -> 4% of each run, Pallas kernels for 32% -> 31%
where the time goes in v3:
time: 91.3 us; the launch traced here: 89.6 us
  starting transfers between devices  29.3 us (32%)
  Pallas kernels  28.2 us (31%)
  waiting for transfers between devices  19.3 us (21%)
  local copies, waits for them, and re-layouts  7.23 us (8%)
  other arithmetic  3.98 us (4%)
  between operations  1.67 us (2%)
    ppermute x16, starting transfers between devices, shards(): came[h][e].append(lax.ppermute(messages[e], 'col', pairs))  27.7 us
    ppermute x16, waiting for transfers between devices, shards(): came[h][e].append(lax.ppermute(messages[e], 'col', pairs))  19.3 us
    pallas_call x2, Pallas kernels, weight_grad(): pl.pallas_call(functools.partial(weight_grad_kernel, h, tile, n), out_sha...  18 us
    unnamed x10, local copies, waits for them, and re-layouts  6.02 us
    pallas_call x1, Pallas kernels, shards(): pl.pallas_call(functools.partial(first_partial_kernel, tile, masks), out_...  5.13 us
    pallas_call x1, Pallas kernels, add_partial(): pl.pallas_call(functools.partial(partial_kernel, h, tile), out_shape=jax....  5 us
  transfers between devices with their start and end apart: 19, of which 4 were waited for; matrix products, arithmetic and copies ran while one was open for 4% of the time, Pallas kernels for 31%

profile of v3, /device:TPU:12, one launch (start us, length us, event | category | flops | bytes accessed | tf_op | source)
XLA Modules:
  0.0 89.6 jit_solution(13298953001639009204)
XLA Ops:
  0.6 0.0 copy-start.3
  0.6 0.0 copy-start.4
  0.6 1.6 %collective-permute-start = (bf16[64,2048]{1,0:T(8,128)(2,1)}, bf16[64,2048]{1,0:T(8,128)(2,1)S(1)}, u32[]{:S(2)}, u32[]{:S(2)}) collective-permute-start(bf16[64,2048]{1,0:T(8,128)(2,1)} %refs_0_.1), channel_id=1, source_target_pairs={{0,8},{4,12},{8,0},{12,4},{1,9},{5,13},{9,1},{13,5},{2,10},{6,14},... | collective-permute-start | bytes 786440 | tf_op jit(solution)/shard_map/ppermute | solution.py:164
  2.2 0.0 collective-permute-start.1
  2.2 1.2 %fusion.1 = (bf16[64,3584]{1,0:T(8,128)(2,1)S(1)}, bf16[64,3584]{1,0:T(8,128)(2,1)S(1)}) fusion(bf16[64,7168]{1,0:T(8,128)(2,1)} %own.3), kind=kLoop, calls=%fused_computation.21 | loop fusion | bytes 1835008 | tf_op jit(solution)/shard_map/slice | solution.py:231
  3.4 3.5 %collective-permute-start.5 = (bf16[64,3584]{1,0:T(8,128)(2,1)S(1)}, bf16[64,3584]{1,0:T(8,128)(2,1)S(1)}, u32[]{:S(2)}, u32[]{:S(2)}) collective-permute-start(bf16[64,3584]{1,0:T(8,128)(2,1)S(1)} %get-tuple-element.38), channel_id=1, source_target_pairs={{1,2},{2,1},{5,6},{6,5},{9,10},{10,9},{13,14},{14,13},{17,18},{18,... | collective-permute-start | bytes 1376264 | tf_op jit(solution)/shard_map/ppermute | solution.py:242
  6.9 0.1 collective-permute-start.6
  7.0 2.0 %collective-permute-start.3 = (bf16[64,3584]{1,0:T(8,128)(2,1)S(1)}, bf16[64,3584]{1,0:T(8,128)(2,1)S(1)}, u32[]{:S(2)}, u32[]{:S(2)}) collective-permute-start(bf16[64,3584]{1,0:T(8,128)(2,1)S(1)} %get-tuple-element.39), channel_id=1, source_target_pairs={{0,1},{1,0},{2,3},{3,2},{4,5},{5,4},{6,7},{7,6},{8,9},{9,8},{10,11... | collective-permute-start | bytes 1376264 | tf_op jit(solution)/shard_map/ppermute | solution.py:242
  9.7 0.0 copy-done.4
  9.7 0.0 collective-permute-done.refs_1_
  9.7 0.1 collective-permute-start.2
  9.8 0.5 select_reduce_fusion.slot_of
  10.3 0.0 collective-permute-done.1.refs_2_
  10.4 2.7 %collective-permute-start.4 = (bf16[64,3584]{1,0:T(8,128)(2,1)S(1)}, bf16[64,3584]{1,0:T(8,128)(2,1)S(1)}, u32[]{:S(2)}, u32[]{:S(2)}) collective-permute-start(bf16[64,3584]{1,0:T(8,128)(2,1)S(1)} %get-tuple-element.39), channel_id=1, source_target_pairs={{1,2},{2,1},{5,6},{6,5},{9,10},{10,9},{13,14},{14,13},{17,18},{18,... | collective-permute-start | bytes 1376264 | tf_op jit(solution)/shard_map/ppermute | solution.py:242
  13.0 0.0 collective-permute-done.2.refs_3_
  13.0 0.0 copy-done.3
  13.0 0.0 copy-start
  13.1 6.0 %copy-done = bf16[1,1,537,128,128]{4,3,2,1,0:T(8,128)(2,1)S(1)} copy-done((bf16[1,1,537,128,128]{4,3,2,1,0:T(8,128)(2,1)S(1)}, bf16[1,1,537,128,128]{4,3,2,1,0:T(8,128)(2,1)}, u32[]{:S(2)}) %copy-start) | copy-done | bytes 17596440
  19.0 0.0 copy-start.1
  19.0 5.1 %partial0.1 = (bf16[256,3584]{1,0:T(8,128)(2,1)S(1)}, bf16[256,2048]{1,0:T(8,128)(2,1)S(1)}) custom-call(s32[896]{0:T(1024)S(1)} %select_reduce_fusion.slot_of, s32[1]{0:T(128)} %bitcast.1.me, bf16[64,2048]{1,0:T(8,128)(2,1)S(1)} %copy-done.3, bf16[64,2048]{1,0:T(8,128)(2,1)S(1)} %collective-permute-done.refs_1_, ...), custom_call_target="tpu_custom_call" | custom-call | flops 3758096384 | bytes 14680064 | tf_op jit(solution)/shard_map/partial0/pallas_call | solution.py:170
  24.2 0.0 collective-permute-done.5.refs_3_
  24.2 0.0 collective-permute-done.6.refs_0_
  24.2 0.4 add_select_fusion.10
  24.6 0.1 collective-permute-start.11
  24.6 3.2 %collective-permute-start.12 = (bf16[64,3584]{1,0:T(8,128)(2,1)S(1)}, bf16[64,3584]{1,0:T(8,128)(2,1)S(1)}, u32[]{:S(2)}, u32[]{:S(2)}) collective-permute-start(bf16[64,3584]{1,0:T(8,128)(2,1)S(1)} %get-tuple-element.36), channel_id=1, source_target_pairs={{1,2},{2,1},{5,6},{6,5},{9,10},{10,9},{13,14},{14,13},{17,18},{18,... | collective-permute-start | bytes 1376264 | tf_op jit(solution)/shard_map/ppermute | solution.py:242
  27.8 0.0 copy-done.1
  27.9 5.0 %partial1.1 = bf16[256,3584]{1,0:T(8,128)(2,1)S(1)} custom-call(s32[896]{0:T(1024)S(1)} %select_reduce_fusion.slot_of, bf16[256,2048]{1,0:T(8,128)(2,1)S(1)} %get-tuple-element.14.grads, bf16[537,128,128]{2,1,0:T(8,128)(2,1)S(1)} %bitcast.10), custom_call_target="tpu_custom_call" | custom-call | flops 3758096384 | bytes 14680064 | tf_op jit(solution)/shard_map/partial1/pallas_call | solution.py:184
  32.9 0.0 collective-permute-done.3.refs_0_
  32.9 0.0 collective-permute-done.4.refs_3_
  32.9 0.3 add_select_fusion.8
  33.2 0.1 collective-permute-start.7
  33.3 2.7 %collective-permute-start.8 = (bf16[64,3584]{1,0:T(8,128)(2,1)S(1)}, bf16[64,3584]{1,0:T(8,128)(2,1)S(1)}, u32[]{:S(2)}, u32[]{:S(2)}) collective-permute-start(bf16[64,3584]{1,0:T(8,128)(2,1)S(1)} %get-tuple-element.32), channel_id=1, source_target_pairs={{1,2},{2,1},{5,6},{6,5},{9,10},{10,9},{13,14},{14,13},{17,18},{18,... | collective-permute-start | bytes 1376264 | tf_op jit(solution)/shard_map/ppermute | solution.py:242
  36.0 4.0 %collective-permute-done.11.refs_1_ = bf16[64,3584]{1,0:T(8,128)(2,1)S(1)} collective-permute-done((bf16[64,3584]{1,0:T(8,128)(2,1)S(1)}, bf16[64,3584]{1,0:T(8,128)(2,1)S(1)}, u32[]{:S(2)}, u32[]{:S(2)}) %collective-permute-start.11) | collective-permute-done | bytes 458784 | tf_op jit(solution)/shard_map/ppermute | solution.py:242
  40.0 0.0 collective-permute-done.12.refs_4_
  40.0 0.3 add_select_fusion.4
  40.3 0.1 collective-permute-start.13
  40.4 3.1 %collective-permute-start.14 = (bf16[64,3584]{1,0:T(8,128)(2,1)S(1)}, bf16[64,3584]{1,0:T(8,128)(2,1)S(1)}, u32[]{:S(2)}, u32[]{:S(2)}) collective-permute-start(bf16[64,3584]{1,0:T(8,128)(2,1)S(1)} %get-tuple-element.34), channel_id=1, source_target_pairs={{1,2},{2,1},{5,6},{6,5},{9,10},{10,9},{13,14},{14,13},{17,18},{18,... | collective-permute-start | bytes 1376264 | tf_op jit(solution)/shard_map/ppermute | solution.py:242
  43.5 6.3 %collective-permute-done.7.refs_1_ = bf16[64,3584]{1,0:T(8,128)(2,1)S(1)} collective-permute-done((bf16[64,3584]{1,0:T(8,128)(2,1)S(1)}, bf16[64,3584]{1,0:T(8,128)(2,1)S(1)}, u32[]{:S(2)}, u32[]{:S(2)}) %collective-permute-start.7) | collective-permute-done | bytes 458784 | tf_op jit(solution)/shard_map/ppermute | solution.py:242
  49.8 0.0 collective-permute-done.8.refs_4_
  49.8 0.3 add_select_fusion.7
  50.2 3.1 %collective-permute-start.10 = (bf16[64,3584]{1,0:T(8,128)(2,1)S(1)}, bf16[64,3584]{1,0:T(8,128)(2,1)S(1)}, u32[]{:S(2)}, u32[]{:S(2)}) collective-permute-start(bf16[64,3584]{1,0:T(8,128)(2,1)S(1)} %get-tuple-element.31), channel_id=1, source_target_pairs={{1,2},{2,1},{5,6},{6,5},{9,10},{10,9},{13,14},{14,13},{17,18},{18,... | collective-permute-start | bytes 1376264 | tf_op jit(solution)/shard_map/ppermute | solution.py:242
  53.3 0.0 copy-start.2
  53.3 0.1 collective-permute-start.9
  53.4 6.3 %collective-permute-done.13.refs_2_ = bf16[64,3584]{1,0:T(8,128)(2,1)S(1)} collective-permute-done((bf16[64,3584]{1,0:T(8,128)(2,1)S(1)}, bf16[64,3584]{1,0:T(8,128)(2,1)S(1)}, u32[]{:S(2)}, u32[]{:S(2)}) %collective-permute-start.13) | collective-permute-done | bytes 458784 | tf_op jit(solution)/shard_map/ppermute | solution.py:242
  59.7 0.0 collective-permute-done.14.refs_5_
  59.7 0.3 constant_dynamic-slice_fusion.1
  60.0 0.1 collective-permute-start.15
  60.1 3.1 %collective-permute-start.16 = (bf16[64,3584]{1,0:T(8,128)(2,1)S(1)}, bf16[64,3584]{1,0:T(8,128)(2,1)S(1)}, u32[]{:S(2)}, u32[]{:S(2)}) collective-permute-start(bf16[64,3584]{1,0:T(8,128)(2,1)S(1)} %get-tuple-element.25.refs_7_), channel_id=1, source_target_pairs={{1,2},{2,1},{5,6},{6,5},{9,10},{10,9},{13,14},{14,13},{17,18},{18,... | collective-permute-start | bytes 1376264 | tf_op jit(solution)/shard_map/ppermute | solution.py:242
  63.2 0.0 copy-done.2
  63.2 7.8 %weight_grad0.1 = (bf16[537,128,128]{2,1,0:T(8,128)(2,1)}, s32[1]{0:T(128)}) custom-call(s32[896]{0:T(1024)S(1)} %select_reduce_fusion.slot_of, s32[1]{0:T(128)} %bitcast.3.where, s32[1]{0:T(128)} %bitcast.7.count, bf16[64,7168]{1,0:T(8,128)(2,1)S(1)} %copy-done.2, bf16[256,2048]{1,0:T(8,128)(2,1)S(1)} %get-tuple-element.14.grads, ...), custom_call_target="tpu_custom_call" | custom-call | flops 3758096384 | bytes 8798208 | tf_op jit(solution)/shard_map/weight_grad0/pallas_call | solution.py:206
  71.0 0.0 collective-permute-done.10.refs_5_
  71.0 0.0 collective-permute-done.9.refs_2_
  71.0 0.3 add_select_fusion
  71.4 0.1 collective-permute-start.17
  71.5 3.9 %collective-permute-start.18 = (bf16[64,3584]{1,0:T(8,128)(2,1)S(1)}, bf16[64,3584]{1,0:T(8,128)(2,1)S(1)}, u32[]{:S(2)}, u32[]{:S(2)}) collective-permute-start(bf16[64,3584]{1,0:T(8,128)(2,1)S(1)} %get-tuple-element.27.refs_7_), channel_id=1, source_target_pairs={{1,2},{2,1},{5,6},{6,5},{9,10},{10,9},{13,14},{14,13},{17,18},{18,... | collective-permute-start | bytes 1376264 | tf_op jit(solution)/shard_map/ppermute | solution.py:242
  75.4 10.2 %weight_grad1.1 = (bf16[537,128,128]{2,1,0:T(8,128)(2,1)}, s32[1]{0:T(128)}) custom-call(s32[896]{0:T(1024)S(1)} %select_reduce_fusion.slot_of, s32[1]{0:T(128)} %bitcast.3.where, s32[1]{0:T(128)} %bitcast.8.count, bf16[64,7168]{1,0:T(8,128)(2,1)S(1)} %copy-done.2, bf16[256,2048]{1,0:T(8,128)(2,1)S(1)} %get-tuple-element.14.grads, ...), custom_call_target="tpu_custom_call", output_to_operand_aliasing={{0}: (13, {})} | custom-call | flops 3758096384 | bytes 8798208 | tf_op jit(solution)/shard_map/weight_grad1/pallas_call | solution.py:206
  85.6 0.0 collective-permute-done.15
  85.7 0.0 collective-permute-done.16
  85.7 0.2 add_convert_fusion.1
  85.9 2.6 %collective-permute-done.17 = bf16[64,3584]{1,0:T(8,128)(2,1)S(1)} collective-permute-done((bf16[64,3584]{1,0:T(8,128)(2,1)S(1)}, bf16[64,3584]{1,0:T(8,128)(2,1)S(1)}, u32[]{:S(2)}, u32[]{:S(2)}) %collective-permute-start.17) | collective-permute-done | bytes 458784 | tf_op jit(solution)/shard_map/ppermute | solution.py:242
  88.5 0.0 collective-permute-done.18
  88.5 0.2 add_convert_fusion
  88.7 1.0 %pad_maximum_fusion = bf16[64,7168]{1,0:T(8,128)(2,1)} fusion(bf16[64,3584]{1,0:T(8,128)(2,1)S(1)} %add_convert_fusion, bf16[64,3584]{1,0:T(8,128)(2,1)S(1)} %add_convert_fusion.1), kind=kLoop, calls=%fused_computation.3 | loop fusion | flops 1835008 | bytes 1835008 | tf_op jit(solution)/shard_map/concatenate | solution.py:256
  (2 shorter events, 0.0 us)
Async XLA Ops:
  0.6 12.4 %copy-start.3 = (bf16[64,2048]{1,0:T(8,128)(2,1)S(1)}, bf16[64,2048]{1,0:T(8,128)(2,1)}, u32[]{:S(2)}) copy-start(bf16[64,2048]{1,0:T(8,128)(2,1)} %refs_0_.1) | copy-start | bytes 786436
  0.6 9.0 %copy-start.4 = (s32[1,1,537]{2,1,0:T(1,128)S(1)}, s32[1,1,537]{2,1,0:T(1,128)}, u32[]{:S(2)}) copy-start(s32[1,1,537]{2,1,0:T(1,128)} %param.8) | copy-start | bytes 6448
  0.6 9.1 %collective-permute-start = (bf16[64,2048]{1,0:T(8,128)(2,1)}, bf16[64,2048]{1,0:T(8,128)(2,1)S(1)}, u32[]{:S(2)}, u32[]{:S(2)}) collective-permute-start(bf16[64,2048]{1,0:T(8,128)(2,1)} %refs_0_.1), channel_id=1, source_target_pairs={{0,8},{4,12},{8,0},{12,4},{1,9},{5,13},{9,1},{13,5},{2,10},{6,14},... | collective-permute-start | bytes 786440 | tf_op jit(solution)/shard_map/ppermute | solution.py:164
  2.2 8.1 %collective-permute-start.1 = (bf16[64,2048]{1,0:T(8,128)(2,1)}, bf16[64,2048]{1,0:T(8,128)(2,1)S(1)}, u32[]{:S(2)}, u32[]{:S(2)}) collective-permute-start(bf16[64,2048]{1,0:T(8,128)(2,1)} %refs_0_.1), channel_id=1, source_target_pairs={{0,4},{4,0},{8,12},{12,8},{1,5},{5,1},{9,13},{13,9},{2,6},{6,2},{1... | collective-permute-start | bytes 786440 | tf_op jit(solution)/shard_map/ppermute | solution.py:164
  3.4 20.8 %collective-permute-start.5 = (bf16[64,3584]{1,0:T(8,128)(2,1)S(1)}, bf16[64,3584]{1,0:T(8,128)(2,1)S(1)}, u32[]{:S(2)}, u32[]{:S(2)}) collective-permute-start(bf16[64,3584]{1,0:T(8,128)(2,1)S(1)} %get-tuple-element.38), channel_id=1, source_target_pairs={{1,2},{2,1},{5,6},{6,5},{9,10},{10,9},{13,14},{14,13},{17,18},{18,... | collective-permute-start | bytes 1376264 | tf_op jit(solution)/shard_map/ppermute | solution.py:242
  6.9 17.3 %collective-permute-start.6 = (bf16[64,3584]{1,0:T(8,128)(2,1)S(1)}, bf16[64,3584]{1,0:T(8,128)(2,1)S(1)}, u32[]{:S(2)}, u32[]{:S(2)}) collective-permute-start(bf16[64,3584]{1,0:T(8,128)(2,1)S(1)} %get-tuple-element.38), channel_id=1, source_target_pairs={{0,1},{1,0},{2,3},{3,2},{4,5},{5,4},{6,7},{7,6},{8,9},{9,8},{10,11... | collective-permute-start | bytes 1376264 | tf_op jit(solution)/shard_map/ppermute | solution.py:242
  7.0 25.9 %collective-permute-start.3 = (bf16[64,3584]{1,0:T(8,128)(2,1)S(1)}, bf16[64,3584]{1,0:T(8,128)(2,1)S(1)}, u32[]{:S(2)}, u32[]{:S(2)}) collective-permute-start(bf16[64,3584]{1,0:T(8,128)(2,1)S(1)} %get-tuple-element.39), channel_id=1, source_target_pairs={{0,1},{1,0},{2,3},{3,2},{4,5},{5,4},{6,7},{7,6},{8,9},{9,8},{10,11... | collective-permute-start | bytes 1376264 | tf_op jit(solution)/shard_map/ppermute | solution.py:242
  9.7 3.3 %collective-permute-start.2 = (bf16[64,2048]{1,0:T(8,128)(2,1)S(1)}, bf16[64,2048]{1,0:T(8,128)(2,1)S(1)}, u32[]{:S(2)}, u32[]{:S(2)}) collective-permute-start(bf16[64,2048]{1,0:T(8,128)(2,1)S(1)} %collective-permute-done.refs_1_), channel_id=1, source_target_pairs={{0,4},{4,0},{8,12},{12,8},{1,5},{5,1},{9,13},{13,9},{2,6},{6,2},{1... | collective-permute-start | bytes 786440 | tf_op jit(solution)/shard_map/ppermute | solution.py:164
  10.4 22.5 %collective-permute-start.4 = (bf16[64,3584]{1,0:T(8,128)(2,1)S(1)}, bf16[64,3584]{1,0:T(8,128)(2,1)S(1)}, u32[]{:S(2)}, u32[]{:S(2)}) collective-permute-start(bf16[64,3584]{1,0:T(8,128)(2,1)S(1)} %get-tuple-element.39), channel_id=1, source_target_pairs={{1,2},{2,1},{5,6},{6,5},{9,10},{10,9},{13,14},{14,13},{17,18},{18,... | collective-permute-start | bytes 1376264 | tf_op jit(solution)/shard_map/ppermute | solution.py:242
  13.0 6.0 %copy-start = (bf16[1,1,537,128,128]{4,3,2,1,0:T(8,128)(2,1)S(1)}, bf16[1,1,537,128,128]{4,3,2,1,0:T(8,128)(2,1)}, u32[]{:S(2)}) copy-start(bf16[1,1,537,128,128]{4,3,2,1,0:T(8,128)(2,1)} %param.7) | copy-start | bytes 52789252
  19.0 8.8 %copy-start.1 = (bf16[1,1,537,128,128]{4,3,2,1,0:T(8,128)(2,1)S(1)}, bf16[1,1,537,128,128]{4,3,2,1,0:T(8,128)(2,1)}, u32[]{:S(2)}) copy-start(bf16[1,1,537,128,128]{4,3,2,1,0:T(8,128)(2,1)} %param.7) | copy-start | bytes 52789252
  24.6 15.4 %collective-permute-start.11 = (bf16[64,3584]{1,0:T(8,128)(2,1)S(1)}, bf16[64,3584]{1,0:T(8,128)(2,1)S(1)}, u32[]{:S(2)}, u32[]{:S(2)}) collective-permute-start(bf16[64,3584]{1,0:T(8,128)(2,1)S(1)} %get-tuple-element.37), channel_id=1, source_target_pairs={{0,1},{1,0},{2,3},{3,2},{4,5},{5,4},{6,7},{7,6},{8,9},{9,8},{10,11... | collective-permute-start | bytes 1376264 | tf_op jit(solution)/shard_map/ppermute | solution.py:242
  24.6 15.4 %collective-permute-start.12 = (bf16[64,3584]{1,0:T(8,128)(2,1)S(1)}, bf16[64,3584]{1,0:T(8,128)(2,1)S(1)}, u32[]{:S(2)}, u32[]{:S(2)}) collective-permute-start(bf16[64,3584]{1,0:T(8,128)(2,1)S(1)} %get-tuple-element.36), channel_id=1, source_target_pairs={{1,2},{2,1},{5,6},{6,5},{9,10},{10,9},{13,14},{14,13},{17,18},{18,... | collective-permute-start | bytes 1376264 | tf_op jit(solution)/shard_map/ppermute | solution.py:242
  33.2 16.6 %collective-permute-start.7 = (bf16[64,3584]{1,0:T(8,128)(2,1)S(1)}, bf16[64,3584]{1,0:T(8,128)(2,1)S(1)}, u32[]{:S(2)}, u32[]{:S(2)}) collective-permute-start(bf16[64,3584]{1,0:T(8,128)(2,1)S(1)} %get-tuple-element.33), channel_id=1, source_target_pairs={{0,1},{1,0},{2,3},{3,2},{4,5},{5,4},{6,7},{7,6},{8,9},{9,8},{10,11... | collective-permute-start | bytes 1376264 | tf_op jit(solution)/shard_map/ppermute | solution.py:242
  33.3 16.5 %collective-permute-start.8 = (bf16[64,3584]{1,0:T(8,128)(2,1)S(1)}, bf16[64,3584]{1,0:T(8,128)(2,1)S(1)}, u32[]{:S(2)}, u32[]{:S(2)}) collective-permute-start(bf16[64,3584]{1,0:T(8,128)(2,1)S(1)} %get-tuple-element.32), channel_id=1, source_target_pairs={{1,2},{2,1},{5,6},{6,5},{9,10},{10,9},{13,14},{14,13},{17,18},{18,... | collective-permute-start | bytes 1376264 | tf_op jit(solution)/shard_map/ppermute | solution.py:242
  40.3 19.3 %collective-permute-start.13 = (bf16[64,3584]{1,0:T(8,128)(2,1)S(1)}, bf16[64,3584]{1,0:T(8,128)(2,1)S(1)}, u32[]{:S(2)}, u32[]{:S(2)}) collective-permute-start(bf16[64,3584]{1,0:T(8,128)(2,1)S(1)} %get-tuple-element.35), channel_id=1, source_target_pairs={{0,1},{1,0},{2,3},{3,2},{4,5},{5,4},{6,7},{7,6},{8,9},{9,8},{10,11... | collective-permute-start | bytes 1376264 | tf_op jit(solution)/shard_map/ppermute | solution.py:242
  40.4 19.2 %collective-permute-start.14 = (bf16[64,3584]{1,0:T(8,128)(2,1)S(1)}, bf16[64,3584]{1,0:T(8,128)(2,1)S(1)}, u32[]{:S(2)}, u32[]{:S(2)}) collective-permute-start(bf16[64,3584]{1,0:T(8,128)(2,1)S(1)} %get-tuple-element.34), channel_id=1, source_target_pairs={{1,2},{2,1},{5,6},{6,5},{9,10},{10,9},{13,14},{14,13},{17,18},{18,... | collective-permute-start | bytes 1376264 | tf_op jit(solution)/shard_map/ppermute | solution.py:242
  50.2 20.8 %collective-permute-start.10 = (bf16[64,3584]{1,0:T(8,128)(2,1)S(1)}, bf16[64,3584]{1,0:T(8,128)(2,1)S(1)}, u32[]{:S(2)}, u32[]{:S(2)}) collective-permute-start(bf16[64,3584]{1,0:T(8,128)(2,1)S(1)} %get-tuple-element.31), channel_id=1, source_target_pairs={{1,2},{2,1},{5,6},{6,5},{9,10},{10,9},{13,14},{14,13},{17,18},{18,... | collective-permute-start | bytes 1376264 | tf_op jit(solution)/shard_map/ppermute | solution.py:242
  53.3 9.9 %copy-start.2 = (bf16[64,7168]{1,0:T(8,128)(2,1)S(1)}, bf16[64,7168]{1,0:T(8,128)(2,1)}, u32[]{:S(2)}) copy-start(bf16[64,7168]{1,0:T(8,128)(2,1)} %own.3) | copy-start | bytes 2752516
  53.3 17.7 %collective-permute-start.9 = (bf16[64,3584]{1,0:T(8,128)(2,1)S(1)}, bf16[64,3584]{1,0:T(8,128)(2,1)S(1)}, u32[]{:S(2)}, u32[]{:S(2)}) collective-permute-start(bf16[64,3584]{1,0:T(8,128)(2,1)S(1)} %get-tuple-element.30), channel_id=1, source_target_pairs={{0,1},{1,0},{2,3},{3,2},{4,5},{5,4},{6,7},{7,6},{8,9},{9,8},{10,11... | collective-permute-start | bytes 1376264 | tf_op jit(solution)/shard_map/ppermute | solution.py:242
  60.0 25.6 %collective-permute-start.15 = (bf16[64,3584]{1,0:T(8,128)(2,1)S(1)}, bf16[64,3584]{1,0:T(8,128)(2,1)S(1)}, u32[]{:S(2)}, u32[]{:S(2)}) collective-permute-start(bf16[64,3584]{1,0:T(8,128)(2,1)S(1)} %get-tuple-element.26.refs_6_), channel_id=1, source_target_pairs={{0,1},{1,0},{2,3},{3,2},{4,5},{5,4},{6,7},{7,6},{8,9},{9,8},{10,11... | collective-permute-start | bytes 1376264 | tf_op jit(solution)/shard_map/ppermute | solution.py:242
  60.1 25.6 %collective-permute-start.16 = (bf16[64,3584]{1,0:T(8,128)(2,1)S(1)}, bf16[64,3584]{1,0:T(8,128)(2,1)S(1)}, u32[]{:S(2)}, u32[]{:S(2)}) collective-permute-start(bf16[64,3584]{1,0:T(8,128)(2,1)S(1)} %get-tuple-element.25.refs_7_), channel_id=1, source_target_pairs={{1,2},{2,1},{5,6},{6,5},{9,10},{10,9},{13,14},{14,13},{17,18},{18,... | collective-permute-start | bytes 1376264 | tf_op jit(solution)/shard_map/ppermute | solution.py:242
  71.4 17.1 %collective-permute-start.17 = (bf16[64,3584]{1,0:T(8,128)(2,1)S(1)}, bf16[64,3584]{1,0:T(8,128)(2,1)S(1)}, u32[]{:S(2)}, u32[]{:S(2)}) collective-permute-start(bf16[64,3584]{1,0:T(8,128)(2,1)S(1)} %get-tuple-element.29.refs_6_), channel_id=1, source_target_pairs={{0,1},{1,0},{2,3},{3,2},{4,5},{5,4},{6,7},{7,6},{8,9},{9,8},{10,11... | collective-permute-start | bytes 1376264 | tf_op jit(solution)/shard_map/ppermute | solution.py:242
  71.5 17.0 %collective-permute-start.18 = (bf16[64,3584]{1,0:T(8,128)(2,1)S(1)}, bf16[64,3584]{1,0:T(8,128)(2,1)S(1)}, u32[]{:S(2)}, u32[]{:S(2)}) collective-permute-start(bf16[64,3584]{1,0:T(8,128)(2,1)S(1)} %get-tuple-element.27.refs_7_), channel_id=1, source_target_pairs={{1,2},{2,1},{5,6},{6,5},{9,10},{10,9},{13,14},{14,13},{17,18},{18,... | collective-permute-start | bytes 1376264 | tf_op jit(solution)/shard_map/ppermute | solution.py:242
